TPU v7x, 512 devices: a whole 4x4x16 slice. The times are simulated.
512 devices in a mesh: ctx: 32 (over x, y, core), exp: 16 (over z).
Axes of the slice: x: 4, y: 4, z: 16, core: 2. Of those that a mesh axis runs over, the one named last changes fastest.
Arguments:
- queries: bfloat16 [1, 8192, 4096], P(None, 'ctx', 'exp'), may hold values from -80 to 80
- keys: bfloat16 [1, 8192, 1024], P(None, 'ctx'), may hold values from -4 to 4
- values: bfloat16 [1, 8192, 1024], P(None, 'ctx'), may hold values from -8 to 8
- routes: int32 [1, 8192, 1], P(None, 'ctx'), may hold values from 0 to 127; in each aligned block of 256 rows (0 to 255, 256 to 511, ..., all dimensions but the last counted through in order) at most 4 rows name the same one
- route_score: float32 [1, 8192], P(None, 'ctx'), may hold values from 0.3 to 1.5
- output_weight: bfloat16 [4096, 4096], P('exp', 'ctx'), may hold values from -0.09375 to 0.09375
- norm_gain: float32 [4096], P('exp'), may hold values from 0.1 to 1.9
- gate_weight: bfloat16 [128, 4096, 512], P('ctx', 'exp'), may hold values from -0.09375 to 0.09375
- up_weight: bfloat16 [128, 4096, 512], P('ctx', 'exp'), may hold values from -0.09375 to 0.09375
- down_weight: bfloat16 [128, 512, 4096], P('ctx', None, 'exp'), may hold values from -0.25 to 0.25
Outputs:
- moe_out: bfloat16 [1, 8192, 4096], P(None, 'ctx', 'exp')
Inputs may be any that keep to these rules, and one draw needn't show every extreme that they name: `routes`: among the 256 tokens at positions j * 256 to j * 256 + 255 of one sequence, at most 4 name the same expert, and 4 is reached.
All inputs are finite; a program needn't handle non-finite values.
Results may differ from a plain program's by a relative error of at most 0.04.
Values may be sent and summed in bfloat16 or wider, within the bound.
A program may use at most 64 MiB of HBM per device.

v0:
```python
import math

import jax
import jax.numpy as jnp
from jax import lax
from jax.sharding import PartitionSpec as P

HD = 128


eps = 1e-05
far_below = -1e30


def attend_keys(state, pieces, query_head_count, query_first, query_last):
    key_portion, value_piece = pieces
    length = key_portion.shape[1]
    width = math.gcd(length, 1024)
    query_count = query_head_count.shape[1]
    positions = query_first + jnp.arange(query_count, dtype=jnp.int32)
    scale = 1.0 / math.sqrt(query_head_count.shape[3])

    def one_block(step, inner):
        block_start = step * width

        def update(carried):
            running, total, summed = carried
            key_tile_block = lax.dynamic_slice_in_dim(key_portion, step * width, width, 1)
            value_block = lax.dynamic_slice_in_dim(value_piece, step * width, width, 1)
            scores = (
                jnp.einsum(
                    "msjp,myp->mjsy",
                    query_head_count,
                    key_tile_block,
                    preferred_element_type=jnp.float32,
                )
                * scale
            )
            key_positions = block_start + jnp.arange(width, dtype=jnp.int32)
            visible = key_positions[None, :] <= positions[:, None]
            scores = jnp.where(visible, scores, far_below)
            newest = jnp.maximum(running, jnp.max(scores, axis=-1))
            weights = jnp.where(visible, jnp.exp(scores - newest[..., None]), 0.0)
            factor = jnp.exp(running - newest)
            total = total * factor + jnp.sum(weights, axis=-1)
            summed = summed * factor[..., None] + jnp.einsum(
                "wump,wpe->wume",
                weights.astype(jnp.bfloat16),
                value_block,
                preferred_element_type=jnp.float32,
            )
            return (newest, total, summed)

        needed = jnp.logical_and(block_start <= query_last, block_start >= 0)
        return lax.cond(needed, update, lambda carried: carried, inner)

    return lax.fori_loop(0, length // width, one_block, state)


def body(
    queries,
    keys,
    values,
    routes,
    route_score,
    output_weight,
    norm_gain,
    gate_weight,
    up_weight,
    down_weight,
):
    batch, tok_rows, local_width = queries.shape
    head_dim = HD
    local_heads = local_width // head_dim
    ctx_size = lax.axis_size("ctx")
    exp_size = lax.axis_size("exp")
    context_index = lax.axis_index("ctx")
    exp_index = lax.axis_index("exp")
    kv_heads = keys.shape[2] // head_dim
    groups = local_heads * exp_size // kv_heads
    kv_head = exp_index * local_heads // groups
    key_mine = lax.dynamic_slice_in_dim(keys, kv_head * head_dim, head_dim, 2)
    value_mine = lax.dynamic_slice_in_dim(values, kv_head * head_dim, head_dim, 2)
    query_head_count = queries.reshape(batch, tok_rows, local_heads, head_dim)
    query_first = context_index * tok_rows
    query_last = query_first + tok_rows - 1
    initial = (
        jnp.full((batch, local_heads, tok_rows), far_below, jnp.float32),
        jnp.zeros((batch, local_heads, tok_rows), jnp.float32),
        jnp.zeros((batch, local_heads, tok_rows, head_dim), jnp.float32),
    )
    running, total, summed = attend_keys(
        initial,
        (
            lax.all_gather(key_mine, "ctx", axis=1, tiled=True),
            lax.all_gather(value_mine, "ctx", axis=1, tiled=True),
        ),
        query_head_count,
        query_first,
        query_last,
    )
    attn = (
        jnp.transpose(summed / total[..., None], (0, 2, 1, 3))
        .reshape(batch, tok_rows, local_width)
        .astype(jnp.bfloat16)
    )
    terms = jnp.einsum(
        "bql,lc->bqc",
        attn,
        lax.all_gather(output_weight, "ctx", axis=1, tiled=True),
        preferred_element_type=jnp.float32,
    )
    projected = lax.psum_scatter(
        terms.astype(jnp.bfloat16), "exp", scatter_dimension=2, tiled=True
    ).astype(jnp.float32)
    local_squares = jnp.sum(projected * projected, axis=-1)
    all_squares = lax.psum(local_squares, "exp")
    model_width = local_width * exp_size
    normed = (projected * lax.rsqrt(all_squares / model_width + eps)[..., None] * norm_gain).astype(
        jnp.bfloat16
    )
    experts_local = gate_weight.shape[0]
    expert_count = experts_local * ctx_size
    most_slots = 2 * tok_rows // expert_count
    chosen = routes[..., 0]
    one_hot = (
        chosen[..., None] == jnp.arange(expert_count, dtype=jnp.int32)[None, None, :]
    ).astype(jnp.float32)
    earlier = (jnp.arange(tok_rows)[:, None] > jnp.arange(tok_rows)[None, :]).astype(jnp.float32)
    before = jnp.einsum("qk,bke->bqe", earlier, one_hot, precision=lax.Precision.HIGHEST)
    rank = jnp.sum(before * one_hot, axis=-1).astype(jnp.int32)
    owner = chosen // experts_local
    local_expert = chosen % experts_local
    sequence = jnp.arange(batch, dtype=jnp.int32)[:, None]
    slot = ((owner * batch + sequence) * most_slots + rank) * experts_local + local_expert
    slot_flat = slot.reshape(-1)
    buffer = jnp.zeros((ctx_size * batch * most_slots * experts_local, local_width), jnp.bfloat16)
    buffer = buffer.at[slot_flat].set(normed.reshape(-1, local_width))
    buffer = buffer.reshape(ctx_size, batch, most_slots, experts_local, local_width)
    arrived = lax.all_to_all(buffer, "ctx", split_axis=0, concat_axis=0, tiled=True)
    routed = arrived.reshape(-1, experts_local, local_width)
    gate_part = jnp.einsum("rel,elf->ref", routed, gate_weight, preferred_element_type=jnp.float32)
    up_part = jnp.einsum("rel,elf->ref", routed, up_weight, preferred_element_type=jnp.float32)
    gate = lax.psum(gate_part.astype(jnp.bfloat16), "exp").astype(jnp.float32)
    upper = lax.psum(up_part.astype(jnp.bfloat16), "exp").astype(jnp.float32)
    hidden = (jax.nn.silu(gate) * upper).astype(jnp.bfloat16)
    produced = jnp.einsum(
        "ref,efl->rel", hidden, down_weight, preferred_element_type=jnp.float32
    ).astype(jnp.bfloat16)
    returned = lax.all_to_all(
        produced.reshape(arrived.shape), "ctx", split_axis=0, concat_axis=0, tiled=True
    )
    expert_out = returned.reshape(-1, local_width)[slot_flat].reshape(batch, tok_rows, local_width)
    scored = route_score[..., None] * expert_out.astype(jnp.float32)
    return scored.astype(jnp.bfloat16)


def solution(mesh):
    placed = (
        P(None, "ctx", "exp"),
        P(None, "ctx", None),
        P(None, "ctx", None),
        P(None, "ctx", None),
        P(None, "ctx"),
        P("exp", "ctx"),
        P("exp"),
        P("ctx", "exp", None),
        P("ctx", "exp", None),
        P("ctx", None, "exp"),
    )
    return jax.shard_map(
        body, mesh=mesh, in_specs=placed, out_specs=P(None, "ctx", "exp"), check_vma=False
    )
```

profile of v0, /device:TPU:1, one launch (start us, length us, event | category | flops | bytes accessed | tf_op | source)
XLA Modules:
  0.0 488.4 jit_solution(11711425704467178275)
XLA Ops:
  6.5 0.0 copy-start
  6.5 0.0 all-gather.4.cloned.1.call-start
  6.5 1.6 constant_dynamic-slice_fusion.1
  8.1 0.0 all-gather.4.cloned.1.call-update
  8.1 0.0 all-gather.6.cloned.1.call-start
  8.2 1.5 constant_dynamic-slice_fusion
  9.7 0.0 all-gather.6.cloned.1.call-update
  9.7 0.0 all-gather.8.cloned.1.call-start
  9.7 0.7 all-gather.8.cloned.1.call-update
  10.4 0.0 reduce-scatter.2.cloned.1.call-start
  10.5 1.0 copy.20
  11.5 0.1 copy.21
  11.6 63.8 %all-gather.4.cloned.1.call-done = bf16[1,8192,128]{2,1,0:T(8,128)(2,1)} async-done(((bf16[1,256,128]{2,1,0:T(8,128)(2,1)}), bf16[1,8192,128]{2,1,0:T(8,128)(2,1)}) %all-gather.4.cloned.1.call-update) | async-done | bytes 2097168 | tf_op jit(solution)/shard_map/all_gather | solution.py:95
  75.4 61.6 %all-gather.6.cloned.1.call-done = bf16[1,8192,128]{2,1,0:T(8,128)(2,1)} async-done(((bf16[1,256,128]{2,1,0:T(8,128)(2,1)}), bf16[1,8192,128]{2,1,0:T(8,128)(2,1)}) %all-gather.6.cloned.1.call-update) | async-done | bytes 2097168 | tf_op jit(solution)/shard_map/all_gather | solution.py:96
  137.1 4.6 while.18
  137.1 4.1 conditional.3
  137.2 0.2 broadcast_compare_fusion
  137.4 1.4 fusion.2
  138.8 1.8 fusion.5
  140.7 0.6 fusion.4
  141.7 0.1 copy.22
  141.8 57.7 %all-gather.8.cloned.1.call-done = bf16[256,4096]{1,0:T(8,128)(2,1)} async-done(((bf16[256,128]{1,0:T(8,128)(2,1)}), bf16[256,4096]{1,0:T(8,128)(2,1)}) %all-gather.8.cloned.1.call-update) | async-done | bytes 2097168 | tf_op jit(solution)/shard_map/all_gather | solution.py:110
  199.5 3.6 fusion.25
  203.1 0.0 reduce-scatter.2.cloned.1.call-update
  203.2 0.0 copy-start.1
  203.2 0.0 all-reduce.3.cloned.1.call-start
  203.2 0.6 copy-done.4
  203.8 0.3 fusion.30
  204.2 61.4 %reduce-scatter.2.cloned.1.call-done = bf16[1,256,256]{2,1,0:T(8,128)(2,1)} async-done(((bf16[1,256,4096]{2,1,0:T(8,128)(2,1)}), bf16[1,256,256]{2,1,0:T(8,128)(2,1)}) %reduce-scatter.2.cloned.1.call-update) | async-done | bytes 131088 | tf_op jit(solution)/shard_map/reduce_scatter | solution.py:113
  265.5 1.0 fusion.38
  266.6 22.4 %psum.21 = f32[1,256]{1,0:T(1,128)S(1)} all-reduce(f32[1,256]{1,0:T(1,128)S(1)} %bitcast.113), channel_id=1, replica_groups=mesh['ctx'=32,'exp'=16] {'exp'}, use_global_device_ids=true, to_apply=%region_9.10 | all-reduce | flops 256 | bytes 2048 | tf_op jit(solution)/shard_map/psum | solution.py:117
  289.0 2.0 scatter_custom_fusion
  291.0 0.1 reshape.352
  291.1 32.5 %all_to_all.10 = bf16[32,1,4,4,256]{4,3,2,1,0:T(4,128)(2,1)S(1)} all-to-all(bf16[32,1,4,4,256]{4,3,2,1,0:T(4,128)(2,1)S(1)} %bitcast.106), channel_id=1, replica_groups=mesh['ctx'=32,'exp'=16] {'ctx'}, dimensions={0} | all-to-all | bytes 524288 | tf_op jit(solution)/shard_map/all_to_all | solution.py:140
  323.6 1.1 fusion.26
  324.7 1.1 fusion.27
  325.8 0.0 all-reduce.3.cloned.1.call-update
  325.8 125.2 %all-reduce.3.cloned.1.call-done = (bf16[128,4,512]{2,0,1:T(8,128)(2,1)}, bf16[128,4,512]{2,0,1:T(8,128)(2,1)}) async-done(((bf16[128,4,512]{2,0,1:T(8,128)(2,1)}, bf16[128,4,512]{2,0,1:T(8,128)(2,1)}), (bf16[128,4,512]{2,0,1:T(8,128)(2,1)}, bf16[128,4,512]{2,0,1:T(8,128)(2,1)})) %all-reduce.3.cloned.1.call-update) | async-done | bytes 1048592 | tf_op jit(solution)/shard_map/psum | solution.py:145
  451.1 1.7 fusion.28
  452.8 0.0 copy-start.3
  452.8 0.1 reshape.354
  452.8 0.8 copy.25
  453.6 17.2 %all-to-all-start.1 = ((bf16[32,1,4,4,256]{4,2,3,1,0:T(4,128)(2,1)}), bf16[32,1,4,4,256]{4,2,3,1,0:T(4,128)(2,1)S(1)}, u32[]{:S(2)}, u32[]{:S(2)}) async-start(bf16[32,1,4,4,256]{4,2,3,1,0:T(4,128)(2,1)} %copy.25), calls=%async_computation.2 | async-start | bytes 524288 | tf_op jit(solution)/shard_map/all_to_all | solution.py:150
  470.8 9.0 %all-to-all-done.1 = bf16[32,1,4,4,256]{4,2,3,1,0:T(4,128)(2,1)S(1)} async-done(((bf16[32,1,4,4,256]{4,2,3,1,0:T(4,128)(2,1)}), bf16[32,1,4,4,256]{4,2,3,1,0:T(4,128)(2,1)S(1)}, u32[]{:S(2)}, u32[]{:S(2)}) %all-to-all-start.1) | async-done | bytes 262176 | tf_op jit(solution)/shard_map/all_to_all | solution.py:150
  479.8 0.1 copy.26
  479.9 0.1 reshape.355
  480.0 1.2 gather_fusion
  481.1 0.8 fusion.41
  (36 shorter events, 0.3 us)
Async XLA Ops:
  6.5 317.0 %copy-start = (bf16[4,256,512]{2,1,0:T(8,128)(2,1)S(1)}, bf16[4,256,512]{2,1,0:T(8,128)(2,1)}, u32[]{:S(2)}) copy-start(bf16[4,256,512]{2,1,0:T(8,128)(2,1)} %param.21) | copy-start | bytes 3145732
  6.5 68.9 %all-gather.4.cloned.1.call-start = ((), (), s32[]{:S(2)}) async-start(), calls=%async_computation.3 | async-start | bytes 2162688 | tf_op jit(solution)/shard_map/all_gather | solution.py:95
  8.1 128.9 %all-gather.6.cloned.1.call-start = ((), (), s32[]{:S(2)}) async-start(), calls=%async_computation.4 | async-start | bytes 2162688 | tf_op jit(solution)/shard_map/all_gather | solution.py:96
  9.7 189.8 %all-gather.8.cloned.1.call-start = ((), (), s32[]{:S(2)}) async-start(), calls=%async_computation.5 | async-start | bytes 2162688 | tf_op jit(solution)/shard_map/all_gather | solution.py:110
  10.4 255.1 %reduce-scatter.2.cloned.1.call-start = ((), (), s32[]{:S(2)}) async-start(), calls=%async_computation.6 | async-start | bytes 2228224 | tf_op jit(solution)/shard_map/reduce_scatter | solution.py:113
  203.1 0.7 copy-start.4
  203.1 85.9 %copy-start.2 = (f32[256]{0:T(256)S(1)}, f32[256]{0:T(256)}, u32[]{:S(2)}) copy-start(f32[256]{0:T(256)} %param.20) | copy-start | bytes 3076
  203.2 121.5 %copy-start.1 = (bf16[4,256,512]{2,1,0:T(8,128)(2,1)S(1)}, bf16[4,256,512]{2,1,0:T(8,128)(2,1)}, u32[]{:S(2)}) copy-start(bf16[4,256,512]{2,1,0:T(8,128)(2,1)} %param.22) | copy-start | bytes 3145732
  203.2 247.9 %all-reduce.3.cloned.1.call-start = ((), (), s32[]{:S(2)}) async-start(), calls=%async_computation.7 | async-start | bytes 2097152 | tf_op jit(solution)/shard_map/psum | solution.py:145
  323.6 127.5 %copy-start.5 = (bf16[4,512,256]{2,1,0:T(8,128)(2,1)S(1)}, bf16[4,512,256]{2,1,0:T(8,128)(2,1)}, u32[]{:S(2)}) copy-start(bf16[4,512,256]{2,1,0:T(8,128)(2,1)} %param.23) | copy-start | bytes 3145732
  452.8 28.4 %copy-start.3 = (f32[1,256]{1,0:T(1,128)S(1)}, f32[1,256]{1,0:T(1,128)}, u32[]{:S(2)}) copy-start(f32[1,256]{1,0:T(1,128)} %param.18) | copy-start | bytes 3076
  453.6 26.2 %all-to-all-start.1 = ((bf16[32,1,4,4,256]{4,2,3,1,0:T(4,128)(2,1)}), bf16[32,1,4,4,256]{4,2,3,1,0:T(4,128)(2,1)S(1)}, u32[]{:S(2)}, u32[]{:S(2)}) async-start(bf16[32,1,4,4,256]{4,2,3,1,0:T(4,128)(2,1)} %copy.25), calls=%async_computation.2 | async-start | bytes 524288 | tf_op jit(solution)/shard_map/all_to_all | solution.py:150
Sparse Core Ops, SparseCore 0:
  10.5 64.8 all-gather.3
  78.5 58.4 all-gather.5
  140.1 59.3 all-gather.7
  203.3 62.1 reduce-scatter.1
  326.0 125.0 all-reduce.2
where the time goes:
time: 489 us; the launch traced here: 488 us
  waiting for transfers between devices  379 us (78%)
  blocking collectives  54.9 us (11%)
  starting transfers between devices  17.4 us (4%)
  between operations  13.3 us (3%)
  matrix products  11.1 us (2%)
  local copies, waits for them, and re-layouts  7.19 us (1%)
    psum x1, waiting for transfers between devices, body(): upper = lax.psum(up_part.astype(jnp.bfloat16), 'exp').astype(jnp.float32)  125 us
    all_gather x1, waiting for transfers between devices, body(): lax.all_gather(key_mine, 'ctx', axis=1, tiled=True)  63.8 us
    all_gather x1, waiting for transfers between devices, body(): lax.all_gather(value_mine, 'ctx', axis=1, tiled=True)  61.6 us
    reduce_scatter x1, waiting for transfers between devices, body(): lax.psum_scatter(terms.astype(jnp.bfloat16), 'exp', scatter_dimension=2,...  61.4 us
    all_gather x1, waiting for transfers between devices, body(): lax.all_gather(output_weight, 'ctx', axis=1, tiled=True)  57.7 us
    all_to_all x1, blocking collectives, body(): lax.all_to_all(buffer, 'ctx', split_axis=0, concat_axis=0, tiled=True)  32.5 us
    psum x1, blocking collectives, body(): all_squares = lax.psum(local_squares, 'exp')  22.4 us
    all_to_all x1, starting transfers between devices, body(): lax.all_to_all(produced.reshape(arrived.shape), 'ctx', split_axis=0, conc...  17.2 us
  transfers between devices with their start and end apart: 6, of which 6 were waited for; matrix products, arithmetic and copies ran while one was open for 1% of the time, Pallas kernels for 0%

commit v1 on v0

v1 whole, which is shorter than its diff:
```python
import functools
import math

import jax
import jax.numpy as jnp
from jax import lax
from jax.experimental import pallas as pl
from jax.experimental.pallas import tpu as pltpu
from jax.sharding import PartitionSpec as P

HD = 128
EPS = 1e-05
FAR_BELOW = -1e30
F32 = jnp.float32
BF16 = jnp.bfloat16
VMEM_LIMIT = 56 * 1024 * 1024


def dot(a, b):
    return jnp.dot(a, b, preferred_element_type=F32)


NX = 4
NY = 4
STEPS_OFF = (0, 1, -1, 2)
MESSAGES = 36
CHUNKS = 4
PARTS = 2


def layer_kernel(
    n_ctx,
    n_exp,
    query_ref,
    route_col_ref,
    route_row_ref,
    gain_ref,
    keys_hbm,
    values_hbm,
    weight_hbm,
    gate_hbm,
    up_hbm,
    down_hbm,
    out_ref,
    kv_ref,
    weight_ref,
    high_ref,
    total_ref,
    attn_ref,
    gu_ref,
    down_ref,
    proj_out,
    proj_in,
    proj_ref,
    packed_ref,
    arrived_ref,
    part_ref,
    gu_out,
    gu_in,
    squares_out,
    squares_in,
    hidden_ref,
    made_ref,
    back_ref,
    load_sem,
    flow_send,
    flow_recv,
    proj_send,
    proj_recv,
    there_send,
    there_recv,
    gu_send,
    gu_recv,
    sq_send,
    sq_recv,
    hid_send,
    hid_recv,
    home_send,
    home_recv,
):
    me = lax.axis_index("ctx")
    z = lax.axis_index("exp")
    half = n_exp // 2
    tokens, local = query_ref.shape
    experts, _, twice = gu_ref.shape
    units = twice // 2
    lots = packed_ref.shape[0]
    each = lots // n_ctx
    most = each // experts
    neighbour = (lax.rem(z + 1, n_exp), lax.rem(z + n_exp - 1, n_exp))

    kv_heads = keys_hbm.shape[1] // HD
    columns = pl.ds(pl.multiple_of(z * kv_heads // n_exp * HD, HD), HD)
    own_loads = [
        pltpu.make_async_copy(keys_hbm.at[:, columns], kv_ref.at[0, me], load_sem.at[3]),
        pltpu.make_async_copy(values_hbm.at[:, columns], kv_ref.at[1, me], load_sem.at[4]),
        pltpu.make_async_copy(weight_hbm, weight_ref.at[me], load_sem.at[5]),
    ]
    for load in own_loads:
        load.start()
    loads = [
        pltpu.make_async_copy(gate_hbm, gu_ref.at[:, :, pl.ds(0, units)], load_sem.at[0]),
        pltpu.make_async_copy(up_hbm, gu_ref.at[:, :, pl.ds(units, units)], load_sem.at[1]),
        pltpu.make_async_copy(down_hbm, down_ref, load_sem.at[2]),
    ]
    for load in loads:
        load.start()

    barrier = pltpu.get_barrier_semaphore()

    def greet_ctx(r, carry):
        pl.semaphore_signal(
            barrier, inc=1, device_id=(lax.rem(me + r, n_ctx), z), device_id_type=pl.DeviceIdType.MESH
        )
        return carry

    def greet_exp(r, carry):
        pl.semaphore_signal(
            barrier, inc=1, device_id=(me, lax.rem(z + r, n_exp)), device_id_type=pl.DeviceIdType.MESH
        )
        return carry

    lax.fori_loop(1, n_ctx, greet_ctx, 0)
    lax.fori_loop(1, n_exp, greet_exp, 0)
    pl.semaphore_wait(barrier, n_ctx - 1 + n_exp - 1)

    def along(source, target, send_sem, recv_sem, way):
        return pltpu.make_async_remote_copy(
            src_ref=source,
            dst_ref=target,
            send_sem=send_sem,
            recv_sem=recv_sem,
            device_id=(me, neighbour[way]),
            device_id_type=pl.DeviceIdType.MESH,
        )

    def target_of(way, step):
        if way == 0:
            return lax.rem(z + half - step, n_exp)
        return lax.rem(z + n_exp - half + step, n_exp)

    lane = me % 2
    chip = me // 2
    at_x, at_y = chip // NY, chip % NY

    def chip_at(dx, dy):
        return lax.rem(at_x + dx + NX, NX) * NY + lax.rem(at_y + dy + NY, NY)

    class Stream:
        def __init__(self, number, ref, first_row, rows, y_first):
            self.number, self.ref, self.first_row, self.rows = number, ref, first_row, rows
            self.y_first = y_first

        def chip(self, da, db):
            return chip_at(db, da) if self.y_first else chip_at(da, db)

        def copy(self, message, da, db, part, to, its_lane=None):
            start, size = self.first_row, self.rows
            if part is not None:
                size = size // 2
                start = start + part * size
            block = self.chip(da, db) * 2 + (lane if its_lane is None else its_lane)
            here = self.ref.at[block, pl.ds(start, size)]
            target = self.chip(0, 0) * 2 + 1 - lane if to is None else self.chip(*to) * 2 + lane
            return pltpu.make_async_remote_copy(
                src_ref=here,
                dst_ref=here,
                send_sem=flow_send.at[self.number, message],
                recv_sem=flow_recv.at[self.number, message],
                device_id=(target, z),
                device_id_type=pl.DeviceIdType.MESH,
            )

        def first(self, side):
            return self.copy(side, 0, 0, None, ((1, 0), (-1, 0))[side])

        def first_in(self, side):
            return self.copy(side, (-1, 1)[side], 0, None, (1, 0))

        def relay(self, side):
            return self.copy(2 + side, (-1, 1)[side], 0, side, ((1, 0), (-1, 0))[side])

        def relay_in(self, side):
            return self.copy(2 + side, 2, 0, side, (1, 0))

        def second(self, i, side):
            return self.copy(4 + 2 * i + side, STEPS_OFF[i], 0, None, ((0, 1), (0, -1))[side])

        def second_in(self, i, side):
            return self.copy(4 + 2 * i + side, STEPS_OFF[i], (-1, 1)[side], None, (0, 1))

        def pass_on(self, i, side):
            return self.copy(
                12 + 2 * i + side, STEPS_OFF[i], (-1, 1)[side], side, ((0, 1), (0, -1))[side]
            )

        def pass_on_in(self, i, side):
            return self.copy(12 + 2 * i + side, STEPS_OFF[i], 2, side, (0, 1))

        def twin(self, i, j):
            return self.copy(20 + 4 * i + j, STEPS_OFF[i], STEPS_OFF[j], None, None)

        def twin_in(self, i, j):
            return self.copy(20 + 4 * i + j, STEPS_OFF[i], STEPS_OFF[j], None, None, 1 - lane)

        def stage(self, number):
            if number == 0:
                for side in range(2):
                    self.first(side).start()
                    self.second(0, side).start()
                self.twin(0, 0).start()
            if number == 1:
                for side in range(2):
                    self.first_in(side).wait_recv()
                    self.relay(side).start()
                    i = 2 - side
                    self.second(i, 0).start()
                    self.second(i, 1).start()
                    self.twin(i, 0).start()
                for side in range(2):
                    self.second_in(0, side).wait_recv()
                    self.pass_on(0, side).start()
                    self.twin(0, 2 - side).start()
            if number == 2:
                for side in range(2):
                    self.relay_in(side).wait_recv()
                for side in range(2):
                    self.second(3, side).start()
                self.twin(3, 0).start()
                for side in range(2):
                    self.pass_on_in(0, side).wait_recv()
                self.twin(0, 3).start()
            if number == 3:
                for i in (1, 2):
                    for side in range(2):
                        self.second_in(i, side).wait_recv()
                        self.pass_on(i, side).start()
                        self.twin(i, 2 - side).start()
            if number == 4:
                for side in range(2):
                    self.second_in(3, side).wait_recv()
                    self.pass_on(3, side).start()
                    self.twin(3, 2 - side).start()
                for i in (1, 2):
                    for side in range(2):
                        self.pass_on_in(i, side).wait_recv()
                    self.twin(i, 3).start()
            if number == 5:
                for side in range(2):
                    self.pass_on_in(3, side).wait_recv()
                self.twin(3, 3).start()

        def sent(self):
            for side in range(2):
                self.first(side).wait_send()
                self.relay(side).wait_send()
                for i in range(4):
                    self.second(i, side).wait_send()
                    self.pass_on(i, side).wait_send()
            for i in range(4):
                for j in range(4):
                    self.twin(i, j).wait_send()

    rows_of_weight = weight_hbm.shape[0]
    key_stream = Stream(0, kv_ref.at[0], 0, tokens, True)
    value_stream = Stream(1, kv_ref.at[1], 0, tokens, False)
    weight_streams = (
        Stream(2, weight_ref, 0, rows_of_weight // 2, True),
        Stream(3, weight_ref, rows_of_weight // 2, rows_of_weight // 2, False),
    )

    def kv_stage(number):
        key_stream.stage(number)
        value_stream.stage(number)

    def weight_stage(number):
        for stream in weight_streams:
            stream.stage(number)

    heads = local // HD
    block = 2 * tokens
    factor = math.log2(math.e) / math.sqrt(HD)

    def attend(dx, dy, own):
        i, j = STEPS_OFF.index(dy), STEPS_OFF.index(dx)
        key_stream.twin_in(i, j).wait_recv()
        value_stream.twin_in(j, i).wait_recv()
        source = chip_at(dx, dy)

        def compute():
            keys = kv_ref[0, pl.ds(source * 2, 2)].reshape(block, HD)
            values = kv_ref[1, pl.ds(source * 2, 2)].reshape(block, HD)
            values = jnp.concatenate([values, jnp.ones((block, HD), BF16)], axis=1)
            for head in range(heads):
                query = query_ref[:, head * HD : (head + 1) * HD]
                scores = lax.dot_general(
                    query, keys, (((1,), (1,)), ((), ())), preferred_element_type=F32
                )
                if own:
                    shape = (tokens, block)
                    spot = lane * tokens + lax.broadcasted_iota(jnp.int32, shape, 0)
                    visible = lax.broadcasted_iota(jnp.int32, shape, 1) <= spot
                    scores = jnp.where(visible, scores, FAR_BELOW)
                highest = jnp.max(scores, axis=1, keepdims=True)
                if not own:
                    before = high_ref[head]
                    highest = jnp.maximum(highest, before)
                weights = jnp.exp2((scores - highest) * factor).astype(BF16)
                summed = dot(weights, values)
                if not own:
                    summed = summed + total_ref[head] * jnp.exp2((before - highest) * factor)
                total_ref[head] = summed
                high_ref[head] = highest

        if own:
            compute()
        else:
            pl.when(source < chip)(compute)

    for load in own_loads:
        load.wait()
    kv_stage(0)
    attend(0, 0, True)
    kv_stage(1)
    for dx, dy in ((0, -1), (-1, 0), (0, 1), (1, 0)):
        attend(dx, dy, False)
    kv_stage(2)
    weight_stage(0)
    for dx, dy in ((0, 2), (2, 0)):
        attend(dx, dy, False)
    kv_stage(3)
    weight_stage(1)
    for dx, dy in ((-1, -1), (-1, 1), (1, -1), (1, 1)):
        attend(dx, dy, False)
    kv_stage(4)
    weight_stage(2)
    for dx, dy in ((2, -1), (2, 1), (-1, 2), (1, 2)):
        attend(dx, dy, False)
    kv_stage(5)
    weight_stage(3)
    attend(2, 2, False)
    weight_stage(4)
    for head in range(heads):
        summed = total_ref[head]
        attn_ref[:, head * HD : (head + 1) * HD] = (summed[:, :HD] / summed[:, HD:]).astype(BF16)
    weight_stage(5)
    for stream in weight_streams:
        for i in range(4):
            for j in range(4):
                stream.twin_in(i, j).wait_recv()

    rows = tokens // CHUNKS
    pairs = n_ctx // n_exp

    def proj_copy(way, step, part):
        spot = pl.ds(part * rows, rows)
        return along(
            proj_out.at[way, step, spot],
            proj_in.at[way, step, spot],
            proj_send.at[way, step, part],
            proj_recv.at[way, step, part],
            way,
        )

    def proj_term(target, part):
        columns = jnp.concatenate(
            [weight_ref[target * pairs + i] for i in range(pairs)], axis=1
        )
        return dot(attn_ref[pl.ds(part * rows, rows), :], columns)

    def far(way, part, parts):
        return (part < parts // 2) == (way == 0)

    def proj_step(step, started):
        for part in range(CHUNKS):
            for way in range(2):
                fresh = started == 0 or (started == 1 and not far(way, part, CHUNKS))
                if started == 0 and not far(way, part, CHUNKS):
                    continue
                spot = pl.ds(part * rows, rows)
                term = proj_term(target_of(way, step), part)
                if not fresh:
                    proj_copy(way, step - 1, part).wait_recv()
                    term = term + proj_in[way, step - 1, spot].astype(F32)
                proj_out[way, step, spot] = term.astype(BF16)
                proj_copy(way, step, part).start()

    proj_step(0, 0)
    proj_step(1, 1)

    def proj_loop(step, carry):
        proj_step(step, 2)
        return carry

    lax.fori_loop(2, half, proj_loop, 0)
    for part in range(CHUNKS):
        spot = pl.ds(part * rows, rows)
        term = proj_term(z, part)
        for way in range(2):
            proj_copy(way, half - 1, part).wait_recv()
            term = term + proj_in[way, half - 1, spot].astype(F32)
        proj_ref[spot, :] = term.astype(BF16)

    chosen_col = route_col_ref[...]
    chosen_row = route_row_ref[...]
    square = (tokens, tokens)
    down_axis = lax.broadcasted_iota(jnp.int32, square, 0)
    over_axis = lax.broadcasted_iota(jnp.int32, square, 1)
    same = chosen_col == chosen_row
    rank_col = jnp.sum(
        jnp.where(same & (over_axis < down_axis), 1.0, 0.0), axis=1, keepdims=True
    ).astype(jnp.int32)
    rank_row = jnp.sum(
        jnp.where(same & (down_axis < over_axis), 1.0, 0.0), axis=0, keepdims=True
    ).astype(jnp.int32)
    slot_col = chosen_col * most + rank_col
    slot_row = chosen_row * most + rank_row
    pick = jnp.where(
        lax.broadcasted_iota(jnp.int32, (lots, tokens), 0) == slot_row, 1.0, 0.0
    ).astype(BF16)
    packed_ref[...] = dot(pick, proj_ref[...]).astype(BF16)

    def there_copy(r):
        peer = lax.rem(me + r, n_ctx)
        return pltpu.make_async_remote_copy(
            src_ref=packed_ref.at[pl.ds(pl.multiple_of(peer * each, each), each)],
            dst_ref=arrived_ref.at[pl.ds(pl.multiple_of(me * each, each), each)],
            send_sem=there_send.at[r],
            recv_sem=there_recv.at[r],
            device_id=(peer, z),
            device_id_type=pl.DeviceIdType.MESH,
        )

    def start_there(r, carry):
        there_copy(r).start()
        return carry

    def wait_there(r, carry):
        there_copy(r).wait_recv()
        return carry

    lax.fori_loop(1, n_ctx, start_there, 0)
    own = pl.ds(pl.multiple_of(me * each, each), each)
    arrived_ref[own, :] = packed_ref[own, :]
    for load in loads:
        load.wait()
    lax.fori_loop(1, n_ctx, wait_there, 0)

    grid = (lots, lots)
    to_row = lax.broadcasted_iota(jnp.int32, grid, 0)
    from_row = lax.broadcasted_iota(jnp.int32, grid, 1)
    in_all = lots // experts
    place = (from_row % each) // most * in_all + from_row // each * most + from_row % most
    by_expert = jnp.where(to_row == place, 1.0, 0.0).astype(BF16)
    tokens_in = dot(by_expert, arrived_ref[...])

    share = lots // n_exp
    squares = lax.dot_general(
        jnp.ones((8, local), F32),
        tokens_in * tokens_in,
        (((1,), (1,)), ((), ())),
        preferred_element_type=F32,
        precision=lax.Precision.HIGHEST,
    )
    for to in range(n_exp):
        squares_out[to, :, pl.ds(0, share)] = squares[0:1, to * share : (to + 1) * share]

    def sq_copy(r):
        peer = lax.rem(z + r, n_exp)
        return pltpu.make_async_remote_copy(
            src_ref=squares_out.at[peer],
            dst_ref=squares_in.at[r],
            send_sem=sq_send.at[r],
            recv_sem=sq_recv.at[r],
            device_id=(me, peer),
            device_id_type=pl.DeviceIdType.MESH,
        )

    def start_sq(r, carry):
        sq_copy(r).start()
        return carry

    lax.fori_loop(1, n_exp, start_sq, 0)

    scaled = (tokens_in * gain_ref[...]).astype(BF16)
    for e in range(experts):
        part_ref[pl.ds(e * in_all, in_all), :] = dot(
            scaled[e * in_all : (e + 1) * in_all, :], gu_ref[e]
        ).astype(BF16)
    piece = share // PARTS

    def gu_copy(way, step, part):
        spot = pl.ds(part * piece, piece)
        return along(
            gu_out.at[way, step, spot],
            gu_in.at[way, step, spot],
            gu_send.at[way, step, part],
            gu_recv.at[way, step, part],
            way,
        )

    def gu_term(target, part):
        return part_ref[pl.ds(pl.multiple_of(target * share + part * piece, piece), piece), :].astype(F32)

    def gu_step(step, started):
        for part in range(PARTS):
            for way in range(2):
                fresh = started == 0 or (started == 1 and not far(way, part, PARTS))
                if started == 0 and not far(way, part, PARTS):
                    continue
                spot = pl.ds(part * piece, piece)
                term = gu_term(target_of(way, step), part)
                if not fresh:
                    gu_copy(way, step - 1, part).wait_recv()
                    term = term + gu_in[way, step - 1, spot].astype(F32)
                gu_out[way, step, spot] = term.astype(BF16)
                gu_copy(way, step, part).start()

    gu_step(0, 0)
    gu_step(1, 1)

    def gu_loop(step, carry):
        gu_step(step, 2)
        return carry

    lax.fori_loop(2, half, gu_loop, 0)

    def wait_sq(r, carry):
        sq_copy(r).wait_recv()
        return carry

    lax.fori_loop(1, n_exp, wait_sq, 0)
    squares_in[0] = squares_out[z]
    row = jnp.sum(squares_in[...], axis=0)
    at_lane = lax.broadcasted_iota(jnp.int32, (share, HD), 1)
    at_row = lax.broadcasted_iota(jnp.int32, (share, HD), 0)
    column = jnp.sum(jnp.where(at_lane == at_row, row, 0.0), axis=1, keepdims=True)
    scale = lax.rsqrt(column / (local * n_exp) + EPS)
    for part in range(PARTS):
        spot = pl.ds(part * piece, piece)
        term = gu_term(z, part)
        for way in range(2):
            gu_copy(way, half - 1, part).wait_recv()
            term = term + gu_in[way, half - 1, spot].astype(F32)
        term = term * scale[part * piece : (part + 1) * piece]
        gate, upper = term[:, :units], term[:, units:]
        hidden = gate / (1.0 + jnp.exp(-gate)) * upper
        hidden_ref[pl.ds(pl.multiple_of(z * share + part * piece, piece), piece), :] = hidden.astype(BF16)

    def hid_copy(way, step):
        block = lax.rem(z + n_exp - step, n_exp) if way == 0 else lax.rem(z + step, n_exp)
        spot = pl.ds(pl.multiple_of(block * share, share), share)
        return along(
            hidden_ref.at[spot], hidden_ref.at[spot], hid_send.at[way, step], hid_recv.at[way, step], way
        )

    def hid_arrival(way, step):
        block = lax.rem(z + n_exp - step - 1, n_exp) if way == 0 else lax.rem(z + step + 1, n_exp)
        spot = pl.ds(pl.multiple_of(block * share, share), share)
        return along(
            hidden_ref.at[spot], hidden_ref.at[spot], hid_send.at[way, step], hid_recv.at[way, step], way
        )

    hid_copy(0, 0).start()
    hid_copy(1, 0).start()

    def hid_loop(step, carry):
        for way in range(2):
            hid_arrival(way, step - 1).wait_recv()
            hid_copy(way, step).start()
        return carry

    lax.fori_loop(1, half - 1, hid_loop, 0)
    hid_arrival(0, half - 2).wait_recv()
    hid_copy(0, half - 1).start()
    hid_arrival(1, half - 2).wait_recv()
    hid_arrival(0, half - 1).wait_recv()

    made = jnp.concatenate(
        [dot(hidden_ref[pl.ds(e * in_all, in_all), :], down_ref[e]) for e in range(experts)], axis=0
    ).astype(BF16)
    place_back = (to_row % each) // most * in_all + to_row // each * most + to_row % most
    by_device = jnp.where(from_row == place_back, 1.0, 0.0).astype(BF16)
    made_ref[...] = dot(by_device, made).astype(BF16)

    def home_copy(r):
        peer = lax.rem(me + r, n_ctx)
        return pltpu.make_async_remote_copy(
            src_ref=made_ref.at[pl.ds(pl.multiple_of(peer * each, each), each)],
            dst_ref=back_ref.at[pl.ds(pl.multiple_of(me * each, each), each)],
            send_sem=home_send.at[r],
            recv_sem=home_recv.at[r],
            device_id=(peer, z),
            device_id_type=pl.DeviceIdType.MESH,
        )

    def start_home(r, carry):
        home_copy(r).start()
        return carry

    def wait_home(r, carry):
        home_copy(r).wait_recv()
        return carry

    lax.fori_loop(1, n_ctx, start_home, 0)
    back_ref[own, :] = made_ref[own, :]

    for stream in (key_stream, value_stream, *weight_streams):
        stream.sent()
    def sent_ctx(r, carry):
        there_copy(r).wait_send()
        home_copy(r).wait_send()
        return carry

    def sent_exp(r, carry):
        sq_copy(r).wait_send()
        return carry

    def sent_ring(step, carry):
        for way in range(2):
            for part in range(CHUNKS):
                proj_copy(way, step, part).wait_send()
            for part in range(PARTS):
                gu_copy(way, step, part).wait_send()
        return carry

    for way in range(2):
        for part in range(CHUNKS):
            if far(way, part, CHUNKS):
                proj_copy(way, 0, part).wait_send()
        for part in range(PARTS):
            if far(way, part, PARTS):
                gu_copy(way, 0, part).wait_send()
    lax.fori_loop(1, half, sent_ring, 0)

    def sent_hid(step, carry):
        for way in range(2):
            hid_copy(way, step).wait_send()
        return carry

    lax.fori_loop(0, half - 1, sent_hid, 0)
    hid_copy(0, half - 1).wait_send()
    lax.fori_loop(1, n_exp, sent_exp, 0)
    lax.fori_loop(1, n_ctx, wait_home, 0)
    lax.fori_loop(1, n_ctx, sent_ctx, 0)

    spread = jnp.where(
        lax.broadcasted_iota(jnp.int32, (tokens, lots), 1) == slot_col, 1.0, 0.0
    ).astype(BF16)
    out_ref[...] = dot(spread, back_ref[...]).astype(BF16)


def layer(n_ctx, n_exp, query, route_col, route_row, gain, keys, values, weight, gate, up, down):
    tokens, local = query.shape
    experts, _, units = gate.shape
    most = 2 * tokens // (experts * n_ctx)
    lots = n_ctx * experts * most
    share = lots // n_exp
    half = n_exp // 2
    heads = local // HD
    dma = pltpu.SemaphoreType.DMA
    vmem = pl.BlockSpec(memory_space=pltpu.VMEM)
    anywhere = pl.BlockSpec(memory_space=pl.ANY)
    return pl.pallas_call(
        functools.partial(layer_kernel, n_ctx, n_exp),
        out_shape=jax.ShapeDtypeStruct((tokens, local), BF16),
        in_specs=[vmem] * 4 + [anywhere] * 6,
        out_specs=vmem,
        scratch_shapes=[
            pltpu.VMEM((2, n_ctx, tokens, HD), BF16),
            pltpu.VMEM((n_ctx, *weight.shape), BF16),
            pltpu.VMEM((heads, tokens, 1), F32),
            pltpu.VMEM((heads, tokens, 2 * HD), F32),
            pltpu.VMEM((tokens, local), BF16),
            pltpu.VMEM((experts, local, 2 * units), BF16),
            pltpu.VMEM((experts, units, local), BF16),
            pltpu.VMEM((2, half, tokens, local), BF16),
            pltpu.VMEM((2, half, tokens, local), BF16),
            pltpu.VMEM((tokens, local), BF16),
            pltpu.VMEM((lots, local), BF16),
            pltpu.VMEM((lots, local), BF16),
            pltpu.VMEM((lots, 2 * units), BF16),
            pltpu.VMEM((2, half, share, 2 * units), BF16),
            pltpu.VMEM((2, half, share, 2 * units), BF16),
            pltpu.VMEM((n_exp, 1, HD), F32),
            pltpu.VMEM((n_exp, 1, HD), F32),
            pltpu.VMEM((lots, units), BF16),
            pltpu.VMEM((lots, local), BF16),
            pltpu.VMEM((lots, local), BF16),
            dma((6,)),
            dma((4, MESSAGES)),
            dma((4, MESSAGES)),
            dma((2, half, CHUNKS)),
            dma((2, half, CHUNKS)),
            dma((n_ctx,)),
            dma((n_ctx,)),
            dma((2, half, PARTS)),
            dma((2, half, PARTS)),
            dma((n_exp,)),
            dma((n_exp,)),
            dma((2, half)),
            dma((2, half)),
            dma((n_ctx,)),
            dma((n_ctx,)),
        ],
        compiler_params=pltpu.CompilerParams(
            collective_id=0, has_side_effects=True, vmem_limit_bytes=VMEM_LIMIT
        ),
        name="layer",
    )(query, route_col, route_row, gain, keys, values, weight, gate, up, down)


def body(
    queries,
    keys,
    values,
    routes,
    route_score,
    output_weight,
    norm_gain,
    gate_weight,
    up_weight,
    down_weight,
):
    tokens, local = queries.shape[1:]
    returned = layer(
        lax.axis_size("ctx"),
        lax.axis_size("exp"),
        queries[0],
        routes[0],
        routes[0].reshape(1, tokens),
        norm_gain.reshape(1, local),
        keys[0],
        values[0],
        output_weight,
        gate_weight,
        up_weight,
        down_weight,
    )
    scored = route_score[0][:, None] * returned.astype(F32)
    return scored.astype(BF16)[None]


def solution(mesh):
    placed = (
        P(None, "ctx", "exp"),
        P(None, "ctx", None),
        P(None, "ctx", None),
        P(None, "ctx", None),
        P(None, "ctx"),
        P("exp", "ctx"),
        P("exp"),
        P("ctx", "exp", None),
        P("ctx", "exp", None),
        P("ctx", None, "exp"),
    )
    return jax.shard_map(
        body, mesh=mesh, in_specs=placed, out_specs=P(None, "ctx", "exp"), check_vma=False
    )
```

time: 489 us -> 156 us (0.32)
  waiting for transfers between devices: 379 us -> 0 us
  Pallas kernels: 0 us -> 153 us
  blocking collectives: 54.9 us -> 0 us
  starting transfers between devices: 17.4 us -> 0 us
  between operations: 13.3 us -> 0.02 us
  matrix products: 11.1 us -> 0 us
  local copies, waits for them, and re-layouts: 7.19 us -> 1.48 us
    all_gather x3 -> x0, waiting for transfers between devices: 183 us -> none  [the longest x1 63.8 us: body(): lax.all_gather(key_mine, 'ctx', axis=1, tiled=True)]
    pallas_call x0 -> x1, Pallas kernels: none -> 153 us  [layer(): pl.pallas_call(functools.partial(layer_kernel, n_ctx, n_exp), out_shape=j...]
    psum x1 -> x0, waiting for transfers between devices: 125 us -> none  [body(): upper = lax.psum(up_part.astype(jnp.bfloat16), 'exp').astype(jnp.float32)]
    reduce_scatter x1 -> x0, waiting for transfers between devices: 61.4 us -> none  [body(): lax.psum_scatter(terms.astype(jnp.bfloat16), 'exp', scatter_dimension=2,...]
    all_to_all x1 -> x0, blocking collectives: 32.5 us -> none  [body(): lax.all_to_all(buffer, 'ctx', split_axis=0, concat_axis=0, tiled=True)]
    psum x1 -> x0, blocking collectives: 22.4 us -> none  [body(): all_squares = lax.psum(local_squares, 'exp')]
    all_to_all x1 -> x0, starting transfers between devices: 17.2 us -> none  [body(): lax.all_to_all(produced.reshape(arrived.shape), 'ctx', split_axis=0, conc...]
    dot_general x7 -> x0, matrix products: 11.1 us -> none  [the longest x1 3.63 us: body(): jnp.einsum('bql,lc->bqc', attn, lax.all_gather(output_weight, 'ctx', axis...]
  transfers between devices with their start and end apart: 6 -> 0, of which waited for: 6 -> 0; matrix products, arithmetic and copies ran while one was open for 1% -> 0% of each run, Pallas kernels for 0% -> 0%
where the time goes in v1:
time: 156 us
  Pallas kernels  153 us (98%)
  other arithmetic  1.66 us (1%)
    pallas_call x1, Pallas kernels, layer(): pl.pallas_call(functools.partial(layer_kernel, n_ctx, n_exp), out_shape=j...  153 us

profile of v1, /device:TPU:1, one launch (start us, length us, event | category | flops | bytes accessed | tf_op | source)
XLA Modules:
  0.0 156.1 jit_solution(15432649982505611454)
XLA Ops:
  0.0 0.0 copy-start
  0.0 0.7 copy-done
  0.7 0.8 copy.11.route_col_ref
  1.5 0.0 copy-start.1
  1.5 152.9 %layer.1 = bf16[256,256]{1,0:T(8,128)(2,1)} custom-call(bf16[256,256]{1,0:T(8,128)(2,1)} %bitcast.11, s32[256,1]{1,0:T(8,128)} %copy.11.route_col_ref, s32[1,256]{1,0:T(1,128)} %bitcast.12, f32[1,256]{1,0:T(1,128)} %bitcast.15, bf16[256,1024]{1,0:T(8,128)(2,1)} %bitcast.9, bf16[256,1024]{1,0:T(8,128)(2,1)} %bitcast.10, bf16[256,128]{1,0:T(8,128)(2,1)} %weight_hbm.1, ...), custom_call_target="tpu_custom_call" | custom-call | tf_op jit(solution)/shard_map/layer/pallas_call | solution.py:664
  154.4 0.0 copy-done.1
  154.4 1.7 %fusion = bf16[1,256,256]{2,1,0:T(8,128)(2,1)} fusion(bf16[256,256]{1,0:T(8,128)(2,1)} %layer.1, f32[256]{0:T(256)S(1)} %bitcast.14), kind=kLoop, calls=%fused_computation.1 | loop fusion | flops 196608 | bytes 263168 | tf_op jit(solution)/shard_map/broadcast_in_dim | solution.py:741
Async XLA Ops:
  0.0 0.7 copy-start
  1.5 153.0 %copy-start.1 = (f32[1,256]{1,0:T(1,128)S(1)}, f32[1,256]{1,0:T(1,128)}, u32[]{:S(2)}) copy-start(f32[1,256]{1,0:T(1,128)} %param.14) | copy-start | bytes 3076

commit v2 on v1

--- a/solution.py
+++ b/solution.py
@@ -32,8 +32,7 @@
     n_ctx,
     n_exp,
     query_ref,
-    route_col_ref,
-    route_row_ref,
+    route_ref,
     gain_ref,
     keys_hbm,
     values_hbm,
@@ -52,8 +51,14 @@
     proj_out,
     proj_in,
     proj_ref,
+    term_ref,
+    pick_ref,
+    spread_ref,
+    by_expert_ref,
+    by_device_ref,
     packed_ref,
     arrived_ref,
+    scaled_ref,
     part_ref,
     gu_out,
     gu_in,
@@ -317,33 +322,68 @@
         else:
             pl.when(source < chip)(compute)
 
+    in_all = lots // experts
+
+    def make_tables():
+        chosen_row = route_ref[...]
+        square = (tokens, tokens)
+        down_axis = lax.broadcasted_iota(jnp.int32, square, 0)
+        over_axis = lax.broadcasted_iota(jnp.int32, square, 1)
+        chosen_col = jnp.sum(
+            jnp.where(down_axis == over_axis, chosen_row.astype(F32), 0.0), axis=1, keepdims=True
+        ).astype(jnp.int32)
+        same = chosen_col == chosen_row
+        rank_col = jnp.sum(
+            jnp.where(same & (over_axis < down_axis), 1.0, 0.0), axis=1, keepdims=True
+        ).astype(jnp.int32)
+        rank_row = jnp.sum(
+            jnp.where(same & (down_axis < over_axis), 1.0, 0.0), axis=0, keepdims=True
+        ).astype(jnp.int32)
+        slot_col = chosen_col * most + rank_col
+        slot_row = chosen_row * most + rank_row
+        pick_ref[...] = jnp.where(
+            lax.broadcasted_iota(jnp.int32, (lots, tokens), 0) == slot_row, 1.0, 0.0
+        ).astype(BF16)
+        spread_ref[...] = jnp.where(
+            lax.broadcasted_iota(jnp.int32, (tokens, lots), 1) == slot_col, 1.0, 0.0
+        ).astype(BF16)
+        lot = lax.broadcasted_iota(jnp.int32, (1, lots), 1)
+        to_row = lax.broadcasted_iota(jnp.int32, (lots, lots), 0)
+        place = (lot % each) // most * in_all + lot // each * most + lot % most
+        by_expert_ref[...] = jnp.where(to_row == place, 1.0, 0.0).astype(BF16)
+        place = (lot % in_all) // most * each + lot // in_all * most + lot % most
+        by_device_ref[...] = jnp.where(to_row == place, 1.0, 0.0).astype(BF16)
+
     for load in own_loads:
         load.wait()
     kv_stage(0)
+    make_tables()
     attend(0, 0, True)
     kv_stage(1)
-    for dx, dy in ((0, -1), (-1, 0), (0, 1), (1, 0)):
+    weight_stage(0)
+    for dx, dy in ((0, -1), (-1, 0)):
         attend(dx, dy, False)
     kv_stage(2)
-    weight_stage(0)
+    for dx, dy in ((0, 1), (1, 0)):
+        attend(dx, dy, False)
+    weight_stage(1)
     for dx, dy in ((0, 2), (2, 0)):
         attend(dx, dy, False)
     kv_stage(3)
-    weight_stage(1)
+    weight_stage(2)
     for dx, dy in ((-1, -1), (-1, 1), (1, -1), (1, 1)):
         attend(dx, dy, False)
     kv_stage(4)
-    weight_stage(2)
+    weight_stage(3)
     for dx, dy in ((2, -1), (2, 1), (-1, 2), (1, 2)):
         attend(dx, dy, False)
     kv_stage(5)
-    weight_stage(3)
+    weight_stage(4)
     attend(2, 2, False)
-    weight_stage(4)
+    weight_stage(5)
     for head in range(heads):
         summed = total_ref[head]
         attn_ref[:, head * HD : (head + 1) * HD] = (summed[:, :HD] / summed[:, HD:]).astype(BF16)
-    weight_stage(5)
     for stream in weight_streams:
         for i in range(4):
             for j in range(4):
@@ -362,11 +402,14 @@
             way,
         )
 
-    def proj_term(target, part):
+    def make_term(target):
         columns = jnp.concatenate(
             [weight_ref[target * pairs + i] for i in range(pairs)], axis=1
         )
-        return dot(attn_ref[pl.ds(part * rows, rows), :], columns)
+        term_ref[target] = dot(attn_ref[...], columns).astype(BF16)
+
+    def proj_term(target, part):
+        return term_ref[target, pl.ds(part * rows, rows)].astype(F32)
 
     def far(way, part, parts):
         return (part < parts // 2) == (way == 0)
@@ -385,14 +428,22 @@
                 proj_out[way, step, spot] = term.astype(BF16)
                 proj_copy(way, step, part).start()
 
+    make_term(target_of(0, 0))
     proj_step(0, 0)
+    make_term(target_of(0, 1))
+    make_term(target_of(1, 1))
     proj_step(1, 1)
 
     def proj_loop(step, carry):
+        make_term(target_of(0, step))
+        make_term(target_of(1, step))
         proj_step(step, 2)
+        for i, stream in enumerate((key_stream, value_stream, *weight_streams)):
+            pl.when(step == 2 + i)(stream.sent)
         return carry
 
     lax.fori_loop(2, half, proj_loop, 0)
+    make_term(z)
     for part in range(CHUNKS):
         spot = pl.ds(part * rows, rows)
         term = proj_term(z, part)
@@ -401,24 +452,7 @@
             term = term + proj_in[way, half - 1, spot].astype(F32)
         proj_ref[spot, :] = term.astype(BF16)
 
-    chosen_col = route_col_ref[...]
-    chosen_row = route_row_ref[...]
-    square = (tokens, tokens)
-    down_axis = lax.broadcasted_iota(jnp.int32, square, 0)
-    over_axis = lax.broadcasted_iota(jnp.int32, square, 1)
-    same = chosen_col == chosen_row
-    rank_col = jnp.sum(
-        jnp.where(same & (over_axis < down_axis), 1.0, 0.0), axis=1, keepdims=True
-    ).astype(jnp.int32)
-    rank_row = jnp.sum(
-        jnp.where(same & (down_axis < over_axis), 1.0, 0.0), axis=0, keepdims=True
-    ).astype(jnp.int32)
-    slot_col = chosen_col * most + rank_col
-    slot_row = chosen_row * most + rank_row
-    pick = jnp.where(
-        lax.broadcasted_iota(jnp.int32, (lots, tokens), 0) == slot_row, 1.0, 0.0
-    ).astype(BF16)
-    packed_ref[...] = dot(pick, proj_ref[...]).astype(BF16)
+    packed_ref[...] = dot(pick_ref[...], proj_ref[...]).astype(BF16)
 
     def there_copy(r):
         peer = lax.rem(me + r, n_ctx)
@@ -446,47 +480,16 @@
         load.wait()
     lax.fori_loop(1, n_ctx, wait_there, 0)
 
-    grid = (lots, lots)
-    to_row = lax.broadcasted_iota(jnp.int32, grid, 0)
-    from_row = lax.broadcasted_iota(jnp.int32, grid, 1)
-    in_all = lots // experts
-    place = (from_row % each) // most * in_all + from_row // each * most + from_row % most
-    by_expert = jnp.where(to_row == place, 1.0, 0.0).astype(BF16)
-    tokens_in = dot(by_expert, arrived_ref[...])
-
     share = lots // n_exp
-    squares = lax.dot_general(
-        jnp.ones((8, local), F32),
-        tokens_in * tokens_in,
-        (((1,), (1,)), ((), ())),
-        preferred_element_type=F32,
-        precision=lax.Precision.HIGHEST,
-    )
-    for to in range(n_exp):
-        squares_out[to, :, pl.ds(0, share)] = squares[0:1, to * share : (to + 1) * share]
-
-    def sq_copy(r):
-        peer = lax.rem(z + r, n_exp)
-        return pltpu.make_async_remote_copy(
-            src_ref=squares_out.at[peer],
-            dst_ref=squares_in.at[r],
-            send_sem=sq_send.at[r],
-            recv_sem=sq_recv.at[r],
-            device_id=(me, peer),
-            device_id_type=pl.DeviceIdType.MESH,
-        )
-
-    def start_sq(r, carry):
-        sq_copy(r).start()
-        return carry
-
-    lax.fori_loop(1, n_exp, start_sq, 0)
-
-    scaled = (tokens_in * gain_ref[...]).astype(BF16)
-    for e in range(experts):
-        part_ref[pl.ds(e * in_all, in_all), :] = dot(
-            scaled[e * in_all : (e + 1) * in_all, :], gu_ref[e]
-        ).astype(BF16)
+    tokens_in = dot(by_expert_ref[...], arrived_ref[...])
+    scaled_ref[...] = (tokens_in * gain_ref[...]).astype(BF16)
+    first_expert = lax.rem(z + half, n_exp) * share // in_all
+
+    def make_part(i):
+        e = lax.rem(first_expert + i, experts)
+        spot = pl.ds(pl.multiple_of(e * in_all, in_all), in_all)
+        part_ref[spot, :] = dot(scaled_ref[spot, :], gu_ref[e]).astype(BF16)
+
     piece = share // PARTS
 
     def gu_copy(way, step, part):
@@ -516,11 +519,43 @@
                 gu_out[way, step, spot] = term.astype(BF16)
                 gu_copy(way, step, part).start()
 
+    make_part(0)
     gu_step(0, 0)
+    for i in range(1, experts):
+        make_part(i)
     gu_step(1, 1)
+
+    squares = lax.dot_general(
+        jnp.ones((8, local), BF16),
+        (tokens_in * tokens_in).astype(BF16),
+        (((1,), (1,)), ((), ())),
+        preferred_element_type=F32,
+    )
+    for to in range(n_exp):
+        squares_out[to, :, pl.ds(0, share)] = squares[0:1, to * share : (to + 1) * share]
+
+    def sq_copy(r):
+        peer = lax.rem(z + r, n_exp)
+        return pltpu.make_async_remote_copy(
+            src_ref=squares_out.at[peer],
+            dst_ref=squares_in.at[r],
+            send_sem=sq_send.at[r],
+            recv_sem=sq_recv.at[r],
+            device_id=(me, peer),
+            device_id_type=pl.DeviceIdType.MESH,
+        )
+
+    def start_sq(r, carry):
+        sq_copy(r).start()
+        return carry
+
+    lax.fori_loop(1, n_exp, start_sq, 0)
 
     def gu_loop(step, carry):
         gu_step(step, 2)
+        for way in range(2):
+            for part in range(CHUNKS):
+                proj_copy(way, step, part).wait_send()
         return carry
 
     lax.fori_loop(2, half, gu_loop, 0)
@@ -547,41 +582,47 @@
         hidden = gate / (1.0 + jnp.exp(-gate)) * upper
         hidden_ref[pl.ds(pl.multiple_of(z * share + part * piece, piece), piece), :] = hidden.astype(BF16)
 
-    def hid_copy(way, step):
-        block = lax.rem(z + n_exp - step, n_exp) if way == 0 else lax.rem(z + step, n_exp)
-        spot = pl.ds(pl.multiple_of(block * share, share), share)
+    def hid_copy(way, step, part, ahead=0):
+        block = lax.rem(z + n_exp - step - ahead, n_exp) if way == 0 else lax.rem(z + step + ahead, n_exp)
+        spot = pl.ds(pl.multiple_of(block * share + part * piece, piece), piece)
         return along(
-            hidden_ref.at[spot], hidden_ref.at[spot], hid_send.at[way, step], hid_recv.at[way, step], way
-        )
-
-    def hid_arrival(way, step):
-        block = lax.rem(z + n_exp - step - 1, n_exp) if way == 0 else lax.rem(z + step + 1, n_exp)
-        spot = pl.ds(pl.multiple_of(block * share, share), share)
-        return along(
-            hidden_ref.at[spot], hidden_ref.at[spot], hid_send.at[way, step], hid_recv.at[way, step], way
-        )
-
-    hid_copy(0, 0).start()
-    hid_copy(1, 0).start()
+            hidden_ref.at[spot],
+            hidden_ref.at[spot],
+            hid_send.at[way, step, part],
+            hid_recv.at[way, step, part],
+            way,
+        )
+
+    def hid_arrival(way, step, part):
+        return hid_copy(way, step, part, 1)
+
+    for part in range(PARTS):
+        hid_copy(0, 0, part).start()
+        hid_copy(1, 0, part).start()
 
     def hid_loop(step, carry):
+        for part in range(PARTS):
+            for way in range(2):
+                hid_arrival(way, step - 1, part).wait_recv()
+                hid_copy(way, step, part).start()
         for way in range(2):
-            hid_arrival(way, step - 1).wait_recv()
-            hid_copy(way, step).start()
+            for part in range(PARTS):
+                gu_copy(way, step, part).wait_send()
         return carry
 
     lax.fori_loop(1, half - 1, hid_loop, 0)
-    hid_arrival(0, half - 2).wait_recv()
-    hid_copy(0, half - 1).start()
-    hid_arrival(1, half - 2).wait_recv()
-    hid_arrival(0, half - 1).wait_recv()
+    for part in range(PARTS):
+        hid_arrival(0, half - 2, part).wait_recv()
+        hid_copy(0, half - 1, part).start()
+    for part in range(PARTS):
+        hid_arrival(1, half - 2, part).wait_recv()
+    for part in range(PARTS):
+        hid_arrival(0, half - 1, part).wait_recv()
 
     made = jnp.concatenate(
         [dot(hidden_ref[pl.ds(e * in_all, in_all), :], down_ref[e]) for e in range(experts)], axis=0
     ).astype(BF16)
-    place_back = (to_row % each) // most * in_all + to_row // each * most + to_row % most
-    by_device = jnp.where(from_row == place_back, 1.0, 0.0).astype(BF16)
-    made_ref[...] = dot(by_device, made).astype(BF16)
+    made_ref[...] = dot(by_device_ref[...], made).astype(BF16)
 
     def home_copy(r):
         peer = lax.rem(me + r, n_ctx)
@@ -605,52 +646,45 @@
     lax.fori_loop(1, n_ctx, start_home, 0)
     back_ref[own, :] = made_ref[own, :]
 
-    for stream in (key_stream, value_stream, *weight_streams):
-        stream.sent()
     def sent_ctx(r, carry):
         there_copy(r).wait_send()
+        return carry
+
+    def sent_home(r, carry):
         home_copy(r).wait_send()
         return carry
 
     def sent_exp(r, carry):
         sq_copy(r).wait_send()
-        return carry
-
-    def sent_ring(step, carry):
-        for way in range(2):
-            for part in range(CHUNKS):
-                proj_copy(way, step, part).wait_send()
-            for part in range(PARTS):
-                gu_copy(way, step, part).wait_send()
         return carry
 
     for way in range(2):
         for part in range(CHUNKS):
             if far(way, part, CHUNKS):
                 proj_copy(way, 0, part).wait_send()
+            proj_copy(way, 1, part).wait_send()
         for part in range(PARTS):
             if far(way, part, PARTS):
                 gu_copy(way, 0, part).wait_send()
-    lax.fori_loop(1, half, sent_ring, 0)
+            gu_copy(way, half - 1, part).wait_send()
 
     def sent_hid(step, carry):
         for way in range(2):
-            hid_copy(way, step).wait_send()
+            for part in range(PARTS):
+                hid_copy(way, step, part).wait_send()
         return carry
 
     lax.fori_loop(0, half - 1, sent_hid, 0)
-    hid_copy(0, half - 1).wait_send()
+    for part in range(PARTS):
+        hid_copy(0, half - 1, part).wait_send()
     lax.fori_loop(1, n_exp, sent_exp, 0)
+    lax.fori_loop(1, n_ctx, sent_ctx, 0)
     lax.fori_loop(1, n_ctx, wait_home, 0)
-    lax.fori_loop(1, n_ctx, sent_ctx, 0)
-
-    spread = jnp.where(
-        lax.broadcasted_iota(jnp.int32, (tokens, lots), 1) == slot_col, 1.0, 0.0
-    ).astype(BF16)
-    out_ref[...] = dot(spread, back_ref[...]).astype(BF16)
-
-
-def layer(n_ctx, n_exp, query, route_col, route_row, gain, keys, values, weight, gate, up, down):
+    out_ref[...] = dot(spread_ref[...], back_ref[...]).astype(BF16)
+    lax.fori_loop(1, n_ctx, sent_home, 0)
+
+
+def layer(n_ctx, n_exp, query, route, gain, keys, values, weight, gate, up, down):
     tokens, local = query.shape
     experts, _, units = gate.shape
     most = 2 * tokens // (experts * n_ctx)
@@ -664,7 +698,7 @@
     return pl.pallas_call(
         functools.partial(layer_kernel, n_ctx, n_exp),
         out_shape=jax.ShapeDtypeStruct((tokens, local), BF16),
-        in_specs=[vmem] * 4 + [anywhere] * 6,
+        in_specs=[vmem] * 3 + [anywhere] * 6,
         out_specs=vmem,
         scratch_shapes=[
             pltpu.VMEM((2, n_ctx, tokens, HD), BF16),
@@ -677,6 +711,12 @@
             pltpu.VMEM((2, half, tokens, local), BF16),
             pltpu.VMEM((2, half, tokens, local), BF16),
             pltpu.VMEM((tokens, local), BF16),
+            pltpu.VMEM((n_exp, tokens, local), BF16),
+            pltpu.VMEM((lots, tokens), BF16),
+            pltpu.VMEM((tokens, lots), BF16),
+            pltpu.VMEM((lots, lots), BF16),
+            pltpu.VMEM((lots, lots), BF16),
+            pltpu.VMEM((lots, local), BF16),
             pltpu.VMEM((lots, local), BF16),
             pltpu.VMEM((lots, local), BF16),
             pltpu.VMEM((lots, 2 * units), BF16),
@@ -698,8 +738,8 @@
             dma((2, half, PARTS)),
             dma((n_exp,)),
             dma((n_exp,)),
-            dma((2, half)),
-            dma((2, half)),
+            dma((2, half, PARTS)),
+            dma((2, half, PARTS)),
             dma((n_ctx,)),
             dma((n_ctx,)),
         ],
@@ -707,7 +747,7 @@
             collective_id=0, has_side_effects=True, vmem_limit_bytes=VMEM_LIMIT
         ),
         name="layer",
-    )(query, route_col, route_row, gain, keys, values, weight, gate, up, down)
+    )(query, route, gain, keys, values, weight, gate, up, down)
 
 
 def body(
@@ -727,7 +767,6 @@
         lax.axis_size("ctx"),
         lax.axis_size("exp"),
         queries[0],
-        routes[0],
         routes[0].reshape(1, tokens),
         norm_gain.reshape(1, local),
         keys[0],

time: 156 us -> 151 us (0.968)
  Pallas kernels: 153 us -> 149 us
    pallas_call x1, Pallas kernels: 153 us -> 149 us  [layer(): pl.pallas_call(functools.partial(layer_kernel, n_ctx, n_exp), out_shape=j...]
where the time goes in v2:
time: 151 us
  Pallas kernels  149 us (99%)
  other arithmetic  1.66 us (1%)
    pallas_call x1, Pallas kernels, layer(): pl.pallas_call(functools.partial(layer_kernel, n_ctx, n_exp), out_shape=j...  149 us

profile of v2, /device:TPU:1, one launch (start us, length us, event | category | flops | bytes accessed | tf_op | source)
XLA Modules:
  0.0 150.6 jit_solution(1340481222870762089)
XLA Ops:
  0.0 0.0 copy-start
  0.0 148.9 %layer.1 = bf16[256,256]{1,0:T(8,128)(2,1)} custom-call(bf16[256,256]{1,0:T(8,128)(2,1)} %bitcast.10, s32[1,256]{1,0:T(1,128)} %bitcast.12, f32[1,256]{1,0:T(1,128)} %bitcast.13, bf16[256,1024]{1,0:T(8,128)(2,1)} %bitcast.8, bf16[256,1024]{1,0:T(8,128)(2,1)} %bitcast.9, bf16[256,128]{1,0:T(8,128)(2,1)} %weight_hbm.1, bf16[4,256,512]{2,1,0:T(8,128)(2,1)} %gate_hbm.1, ...), custom_call_target="tpu_custom_call" | custom-call | tf_op jit(solution)/shard_map/layer/pallas_call | solution.py:698
  148.9 0.0 copy-done
  148.9 1.7 %fusion = bf16[1,256,256]{2,1,0:T(8,128)(2,1)} fusion(bf16[256,256]{1,0:T(8,128)(2,1)} %layer.1, f32[256]{0:T(256)S(1)} %bitcast.11), kind=kLoop, calls=%fused_computation.1 | loop fusion | flops 196608 | bytes 263168 | tf_op jit(solution)/shard_map/broadcast_in_dim | solution.py:780
Async XLA Ops:
  0.0 148.9 %copy-start = (f32[1,256]{1,0:T(1,128)S(1)}, f32[1,256]{1,0:T(1,128)}, u32[]{:S(2)}) copy-start(f32[1,256]{1,0:T(1,128)} %param.14) | copy-start | bytes 3076

commit v3 on v2

--- a/solution.py
+++ b/solution.py
@@ -492,38 +492,82 @@
 
     piece = share // PARTS
 
-    def gu_copy(way, step, part):
+    hops = half // 2
+
+    def place_at(way, offset):
+        return lax.rem(z + (offset if way == 0 else n_exp - offset), n_exp)
+
+    def move(source, target, send_sem, recv_sem, way, distance):
+        return pltpu.make_async_remote_copy(
+            src_ref=source,
+            dst_ref=target,
+            send_sem=send_sem,
+            recv_sem=recv_sem,
+            device_id=(me, place_at(way, distance)),
+            device_id_type=pl.DeviceIdType.MESH,
+        )
+
+    def part_rows(target, part):
+        return pl.ds(pl.multiple_of(target * share + part * piece, piece), piece)
+
+    def gu_chain(way, step, part):
         spot = pl.ds(part * piece, piece)
-        return along(
-            gu_out.at[way, step, spot],
+        if step == 0:
+            source = part_ref.at[part_rows(place_at(way, half), part)]
+        else:
+            source = gu_out.at[way, step, spot]
+        return move(
+            source,
             gu_in.at[way, step, spot],
             gu_send.at[way, step, part],
             gu_recv.at[way, step, part],
             way,
+            2,
+        )
+
+    def gu_leaf(way, step, part):
+        spot = pl.ds(part * piece, piece)
+        return move(
+            part_ref.at[part_rows(place_at(way, half - 1 - 2 * step), part)],
+            gu_in.at[way, hops + step, spot],
+            gu_send.at[way, hops + step, part],
+            gu_recv.at[way, hops + step, part],
+            way,
+            1,
         )
 
     def gu_term(target, part):
-        return part_ref[pl.ds(pl.multiple_of(target * share + part * piece, piece), piece), :].astype(F32)
-
-    def gu_step(step, started):
-        for part in range(PARTS):
-            for way in range(2):
-                fresh = started == 0 or (started == 1 and not far(way, part, PARTS))
-                if started == 0 and not far(way, part, PARTS):
-                    continue
-                spot = pl.ds(part * piece, piece)
-                term = gu_term(target_of(way, step), part)
-                if not fresh:
-                    gu_copy(way, step - 1, part).wait_recv()
-                    term = term + gu_in[way, step - 1, spot].astype(F32)
-                gu_out[way, step, spot] = term.astype(BF16)
-                gu_copy(way, step, part).start()
+        return part_ref[part_rows(target, part), :].astype(F32)
+
+    def gu_arrived(term, way, step, part):
+        spot = pl.ds(part * piece, piece)
+        gu_leaf(way, step, part).wait_recv()
+        term = term + gu_in[way, hops + step, spot].astype(F32)
+        if step > 0 or far(way, part, PARTS):
+            gu_chain(way, step, part).wait_recv()
+            term = term + gu_in[way, step, spot].astype(F32)
+        return term
+
+    both = [(way, part) for part in range(PARTS) for way in range(2)]
+
+    def gu_leaves(step):
+        for way, part in both:
+            gu_leaf(way, step, part).start()
+
+    def gu_step(step):
+        gu_leaves(step)
+        for way, part in both:
+            term = gu_arrived(gu_term(place_at(way, half - 2 * step), part), way, step - 1, part)
+            gu_out[way, step, pl.ds(part * piece, piece)] = term.astype(BF16)
+            gu_chain(way, step, part).start()
 
     make_part(0)
-    gu_step(0, 0)
+    for way, part in both:
+        if far(way, part, PARTS):
+            gu_chain(way, 0, part).start()
     for i in range(1, experts):
         make_part(i)
-    gu_step(1, 1)
+    gu_leaves(0)
 
     squares = lax.dot_general(
         jnp.ones((8, local), BF16),
@@ -551,14 +595,18 @@
 
     lax.fori_loop(1, n_exp, start_sq, 0)
 
-    def gu_loop(step, carry):
-        gu_step(step, 2)
+    def sent_proj(step, carry):
         for way in range(2):
             for part in range(CHUNKS):
                 proj_copy(way, step, part).wait_send()
         return carry
 
-    lax.fori_loop(2, half, gu_loop, 0)
+    for step in range(1, hops):
+        gu_step(step)
+        if step == 1:
+            lax.fori_loop(1, half // 2, sent_proj, 0)
+        if step == 2:
+            lax.fori_loop(half // 2, half, sent_proj, 0)
 
     def wait_sq(r, carry):
         sq_copy(r).wait_recv()
@@ -572,52 +620,47 @@
     column = jnp.sum(jnp.where(at_lane == at_row, row, 0.0), axis=1, keepdims=True)
     scale = lax.rsqrt(column / (local * n_exp) + EPS)
     for part in range(PARTS):
-        spot = pl.ds(part * piece, piece)
         term = gu_term(z, part)
         for way in range(2):
-            gu_copy(way, half - 1, part).wait_recv()
-            term = term + gu_in[way, half - 1, spot].astype(F32)
+            term = gu_arrived(term, way, hops - 1, part)
         term = term * scale[part * piece : (part + 1) * piece]
         gate, upper = term[:, :units], term[:, units:]
         hidden = gate / (1.0 + jnp.exp(-gate)) * upper
         hidden_ref[pl.ds(pl.multiple_of(z * share + part * piece, piece), piece), :] = hidden.astype(BF16)
 
-    def hid_copy(way, step, part, ahead=0):
-        block = lax.rem(z + n_exp - step - ahead, n_exp) if way == 0 else lax.rem(z + step + ahead, n_exp)
-        spot = pl.ds(pl.multiple_of(block * share + part * piece, piece), piece)
-        return along(
-            hidden_ref.at[spot],
-            hidden_ref.at[spot],
-            hid_send.at[way, step, part],
-            hid_recv.at[way, step, part],
-            way,
-        )
-
-    def hid_arrival(way, step, part):
-        return hid_copy(way, step, part, 1)
-
-    for part in range(PARTS):
-        hid_copy(0, 0, part).start()
-        hid_copy(1, 0, part).start()
-
-    def hid_loop(step, carry):
-        for part in range(PARTS):
-            for way in range(2):
-                hid_arrival(way, step - 1, part).wait_recv()
-                hid_copy(way, step, part).start()
-        for way in range(2):
-            for part in range(PARTS):
-                gu_copy(way, step, part).wait_send()
-        return carry
-
-    lax.fori_loop(1, half - 1, hid_loop, 0)
-    for part in range(PARTS):
-        hid_arrival(0, half - 2, part).wait_recv()
-        hid_copy(0, half - 1, part).start()
-    for part in range(PARTS):
-        hid_arrival(1, half - 2, part).wait_recv()
-    for part in range(PARTS):
-        hid_arrival(0, half - 1, part).wait_recv()
+    def hid_copy(way, step, part, distance, ahead=0):
+        block = place_at(1 - way, 2 * step + ahead)
+        spot = hidden_ref.at[part_rows(block, part)]
+        lane_of = (2 - distance) * hops + step
+        return move(
+            spot, spot, hid_send.at[way, lane_of, part], hid_recv.at[way, lane_of, part], way, distance
+        )
+
+    def hid_far(way, step, part):
+        return step < hops - 1 or far(way, part, PARTS)
+
+    for step in range(hops):
+        for way, part in both:
+            if step > 0:
+                hid_copy(way, step - 1, part, 2, 2).wait_recv()
+            if hid_far(way, step, part):
+                hid_copy(way, step, part, 2).start()
+            hid_copy(way, step, part, 1).start()
+        if step == 0:
+            for way, part in both:
+                if far(way, part, PARTS):
+                    gu_chain(way, 0, part).wait_send()
+                gu_leaf(way, 0, part).wait_send()
+        else:
+            for way, part in both:
+                gu_chain(way, step, part).wait_send()
+                gu_leaf(way, step, part).wait_send()
+    for step in range(hops):
+        for way, part in both:
+            hid_copy(way, step, part, 1, 1).wait_recv()
+    for way, part in both:
+        if hid_far(way, hops - 1, part):
+            hid_copy(way, hops - 1, part, 2, 2).wait_recv()
 
     made = jnp.concatenate(
         [dot(hidden_ref[pl.ds(e * in_all, in_all), :], down_ref[e]) for e in range(experts)], axis=0
@@ -662,21 +705,11 @@
         for part in range(CHUNKS):
             if far(way, part, CHUNKS):
                 proj_copy(way, 0, part).wait_send()
-            proj_copy(way, 1, part).wait_send()
-        for part in range(PARTS):
-            if far(way, part, PARTS):
-                gu_copy(way, 0, part).wait_send()
-            gu_copy(way, half - 1, part).wait_send()
-
-    def sent_hid(step, carry):
-        for way in range(2):
-            for part in range(PARTS):
-                hid_copy(way, step, part).wait_send()
-        return carry
-
-    lax.fori_loop(0, half - 1, sent_hid, 0)
-    for part in range(PARTS):
-        hid_copy(0, half - 1, part).wait_send()
+    for step in range(hops):
+        for way, part in both:
+            if hid_far(way, step, part):
+                hid_copy(way, step, part, 2).wait_send()
+            hid_copy(way, step, part, 1).wait_send()
     lax.fori_loop(1, n_exp, sent_exp, 0)
     lax.fori_loop(1, n_ctx, sent_ctx, 0)
     lax.fori_loop(1, n_ctx, wait_home, 0)

time: 151 us -> 135 us (0.89)
  Pallas kernels: 149 us -> 133 us
    pallas_call x1, Pallas kernels: 149 us -> 133 us  [layer(): pl.pallas_call(functools.partial(layer_kernel, n_ctx, n_exp), out_shape=j...]
where the time goes in v3:
time: 135 us
  Pallas kernels  133 us (99%)
  other arithmetic  1.66 us (1%)
    pallas_call x1, Pallas kernels, layer(): pl.pallas_call(functools.partial(layer_kernel, n_ctx, n_exp), out_shape=j...  133 us

profile of v3, /device:TPU:1, one launch (start us, length us, event | category | flops | bytes accessed | tf_op | source)
XLA Modules:
  0.0 134.5 jit_solution(5015736432902372420)
XLA Ops:
  0.0 0.0 copy-start
  0.0 132.8 %layer.1 = bf16[256,256]{1,0:T(8,128)(2,1)} custom-call(bf16[256,256]{1,0:T(8,128)(2,1)} %bitcast.10, s32[1,256]{1,0:T(1,128)} %bitcast.12, f32[1,256]{1,0:T(1,128)} %bitcast.13, bf16[256,1024]{1,0:T(8,128)(2,1)} %bitcast.8, bf16[256,1024]{1,0:T(8,128)(2,1)} %bitcast.9, bf16[256,128]{1,0:T(8,128)(2,1)} %weight_hbm.1, bf16[4,256,512]{2,1,0:T(8,128)(2,1)} %gate_hbm.1, ...), custom_call_target="tpu_custom_call" | custom-call | tf_op jit(solution)/shard_map/layer/pallas_call | solution.py:731
  132.8 0.0 copy-done
  132.9 1.7 %fusion = bf16[1,256,256]{2,1,0:T(8,128)(2,1)} fusion(bf16[256,256]{1,0:T(8,128)(2,1)} %layer.1, f32[256]{0:T(256)S(1)} %bitcast.11), kind=kLoop, calls=%fused_computation.1 | loop fusion | flops 196608 | bytes 263168 | tf_op jit(solution)/shard_map/broadcast_in_dim | solution.py:813
Async XLA Ops:
  0.0 132.9 %copy-start = (f32[1,256]{1,0:T(1,128)S(1)}, f32[1,256]{1,0:T(1,128)}, u32[]{:S(2)}) copy-start(f32[1,256]{1,0:T(1,128)} %param.14) | copy-start | bytes 3076

commit v4 on v3

--- a/solution.py
+++ b/solution.py
@@ -92,13 +92,12 @@
     lots = packed_ref.shape[0]
     each = lots // n_ctx
     most = each // experts
-    neighbour = (lax.rem(z + 1, n_exp), lax.rem(z + n_exp - 1, n_exp))
 
     kv_heads = keys_hbm.shape[1] // HD
     columns = pl.ds(pl.multiple_of(z * kv_heads // n_exp * HD, HD), HD)
     own_loads = [
-        pltpu.make_async_copy(keys_hbm.at[:, columns], kv_ref.at[0, me], load_sem.at[3]),
-        pltpu.make_async_copy(values_hbm.at[:, columns], kv_ref.at[1, me], load_sem.at[4]),
+        pltpu.make_async_copy(keys_hbm.at[:, columns], kv_ref.at[me, 0], load_sem.at[3]),
+        pltpu.make_async_copy(values_hbm.at[:, columns], kv_ref.at[me, 1], load_sem.at[4]),
         pltpu.make_async_copy(weight_hbm, weight_ref.at[me], load_sem.at[5]),
     ]
     for load in own_loads:
@@ -129,21 +128,6 @@
     lax.fori_loop(1, n_exp, greet_exp, 0)
     pl.semaphore_wait(barrier, n_ctx - 1 + n_exp - 1)
 
-    def along(source, target, send_sem, recv_sem, way):
-        return pltpu.make_async_remote_copy(
-            src_ref=source,
-            dst_ref=target,
-            send_sem=send_sem,
-            recv_sem=recv_sem,
-            device_id=(me, neighbour[way]),
-            device_id_type=pl.DeviceIdType.MESH,
-        )
-
-    def target_of(way, step):
-        if way == 0:
-            return lax.rem(z + half - step, n_exp)
-        return lax.rem(z + n_exp - half + step, n_exp)
-
     lane = me % 2
     chip = me // 2
     at_x, at_y = chip // NY, chip % NY
@@ -152,21 +136,19 @@
         return lax.rem(at_x + dx + NX, NX) * NY + lax.rem(at_y + dy + NY, NY)
 
     class Stream:
-        def __init__(self, number, ref, first_row, rows, y_first):
-            self.number, self.ref, self.first_row, self.rows = number, ref, first_row, rows
-            self.y_first = y_first
+        def __init__(self, number, ref, size):
+            self.number, self.ref, self.size = number, ref, size
 
         def chip(self, da, db):
-            return chip_at(db, da) if self.y_first else chip_at(da, db)
-
-        def copy(self, message, da, db, part, to, its_lane=None):
-            start, size = self.first_row, self.rows
+            return chip_at(lane * da + (1 - lane) * db, lane * db + (1 - lane) * da)
+
+        def copy(self, message, da, db, part, to, twin=False):
+            block = self.chip(da, db) * 2 + (1 - lane if twin else lane)
+            half_size = self.size // 2
+            here = self.ref.at[block]
             if part is not None:
-                size = size // 2
-                start = start + part * size
-            block = self.chip(da, db) * 2 + (lane if its_lane is None else its_lane)
-            here = self.ref.at[block, pl.ds(start, size)]
-            target = self.chip(0, 0) * 2 + 1 - lane if to is None else self.chip(*to) * 2 + lane
+                here = self.ref.at[block, pl.ds(part * half_size, half_size)]
+            target = chip * 2 + 1 - lane if to is None else self.chip(*to) * 2 + lane
             return pltpu.make_async_remote_copy(
                 src_ref=here,
                 dst_ref=here,
@@ -206,26 +188,27 @@
             return self.copy(20 + 4 * i + j, STEPS_OFF[i], STEPS_OFF[j], None, None)
 
         def twin_in(self, i, j):
-            return self.copy(20 + 4 * i + j, STEPS_OFF[i], STEPS_OFF[j], None, None, 1 - lane)
+            return self.copy(20 + 4 * j + i, STEPS_OFF[i], STEPS_OFF[j], None, None, True)
 
         def stage(self, number):
             if number == 0:
                 for side in range(2):
                     self.first(side).start()
+                self.twin(0, 0).start()
+                for side in range(2):
                     self.second(0, side).start()
-                self.twin(0, 0).start()
             if number == 1:
                 for side in range(2):
                     self.first_in(side).wait_recv()
                     self.relay(side).start()
-                    i = 2 - side
-                    self.second(i, 0).start()
-                    self.second(i, 1).start()
-                    self.twin(i, 0).start()
+                    self.twin(2 - side, 0).start()
                 for side in range(2):
                     self.second_in(0, side).wait_recv()
                     self.pass_on(0, side).start()
                     self.twin(0, 2 - side).start()
+                for i in (2, 1):
+                    for side in range(2):
+                        self.second(i, side).start()
             if number == 2:
                 for side in range(2):
                     self.relay_in(side).wait_recv()
@@ -266,35 +249,25 @@
                 for j in range(4):
                     self.twin(i, j).wait_send()
 
-    rows_of_weight = weight_hbm.shape[0]
-    key_stream = Stream(0, kv_ref.at[0], 0, tokens, True)
-    value_stream = Stream(1, kv_ref.at[1], 0, tokens, False)
-    weight_streams = (
-        Stream(2, weight_ref, 0, rows_of_weight // 2, True),
-        Stream(3, weight_ref, rows_of_weight // 2, rows_of_weight // 2, False),
-    )
-
-    def kv_stage(number):
-        key_stream.stage(number)
-        value_stream.stage(number)
-
-    def weight_stage(number):
-        for stream in weight_streams:
-            stream.stage(number)
+    kv_stream = Stream(0, kv_ref, 2)
+    weight_stream = Stream(1, weight_ref, weight_hbm.shape[0])
+
+    def stage(number):
+        kv_stream.stage(number)
+        weight_stream.stage(number)
 
     heads = local // HD
     block = 2 * tokens
     factor = math.log2(math.e) / math.sqrt(HD)
 
-    def attend(dx, dy, own):
-        i, j = STEPS_OFF.index(dy), STEPS_OFF.index(dx)
-        key_stream.twin_in(i, j).wait_recv()
-        value_stream.twin_in(j, i).wait_recv()
-        source = chip_at(dx, dy)
+    def attend(i, j):
+        own = i == 0 and j == 0
+        kv_stream.twin_in(i, j).wait_recv()
+        source = kv_stream.chip(STEPS_OFF[i], STEPS_OFF[j])
 
         def compute():
-            keys = kv_ref[0, pl.ds(source * 2, 2)].reshape(block, HD)
-            values = kv_ref[1, pl.ds(source * 2, 2)].reshape(block, HD)
+            keys = kv_ref[pl.ds(source * 2, 2), 0].reshape(block, HD)
+            values = kv_ref[pl.ds(source * 2, 2), 1].reshape(block, HD)
             values = jnp.concatenate([values, jnp.ones((block, HD), BF16)], axis=1)
             for head in range(heads):
                 query = query_ref[:, head * HD : (head + 1) * HD]
@@ -356,50 +329,76 @@
 
     for load in own_loads:
         load.wait()
-    kv_stage(0)
+    stage(0)
     make_tables()
-    attend(0, 0, True)
-    kv_stage(1)
-    weight_stage(0)
-    for dx, dy in ((0, -1), (-1, 0)):
-        attend(dx, dy, False)
-    kv_stage(2)
-    for dx, dy in ((0, 1), (1, 0)):
-        attend(dx, dy, False)
-    weight_stage(1)
-    for dx, dy in ((0, 2), (2, 0)):
-        attend(dx, dy, False)
-    kv_stage(3)
-    weight_stage(2)
-    for dx, dy in ((-1, -1), (-1, 1), (1, -1), (1, 1)):
-        attend(dx, dy, False)
-    kv_stage(4)
-    weight_stage(3)
-    for dx, dy in ((2, -1), (2, 1), (-1, 2), (1, 2)):
-        attend(dx, dy, False)
-    kv_stage(5)
-    weight_stage(4)
-    attend(2, 2, False)
-    weight_stage(5)
+    attend(0, 0)
+    stage(1)
+    stage(2)
+    for i, j in ((1, 0), (2, 0), (0, 1), (0, 2)):
+        attend(i, j)
+    stage(3)
+    for i, j in ((3, 0), (0, 3)):
+        attend(i, j)
+    stage(4)
+    for i, j in ((1, 1), (1, 2), (2, 1), (2, 2)):
+        attend(i, j)
+    stage(5)
+    for i, j in ((3, 1), (3, 2), (1, 3), (2, 3), (3, 3)):
+        attend(i, j)
     for head in range(heads):
         summed = total_ref[head]
         attn_ref[:, head * HD : (head + 1) * HD] = (summed[:, :HD] / summed[:, HD:]).astype(BF16)
-    for stream in weight_streams:
-        for i in range(4):
-            for j in range(4):
-                stream.twin_in(i, j).wait_recv()
+    for i in range(4):
+        for j in range(4):
+            weight_stream.twin_in(i, j).wait_recv()
 
     rows = tokens // CHUNKS
     pairs = n_ctx // n_exp
 
+    def place_at(way, offset):
+        return lax.rem(z + (offset if way == 0 else n_exp - offset), n_exp)
+
+    def move(source, target, send_sem, recv_sem, way, distance):
+        return pltpu.make_async_remote_copy(
+            src_ref=source,
+            dst_ref=target,
+            send_sem=send_sem,
+            recv_sem=recv_sem,
+            device_id=(me, place_at(way, distance)),
+            device_id_type=pl.DeviceIdType.MESH,
+        )
+
+    def proj_far(way, part):
+        spot = pl.ds(part * rows, rows)
+        return move(
+            term_ref.at[place_at(way, half), spot],
+            proj_in.at[way, 0, spot],
+            proj_send.at[way, 0, part],
+            proj_recv.at[way, 0, part],
+            way,
+            2,
+        )
+
+    def proj_near(way, part):
+        spot = pl.ds(part * rows, rows)
+        return move(
+            term_ref.at[place_at(way, half - 1), spot],
+            proj_in.at[way, half - 1, spot],
+            proj_send.at[way, half - 1, part],
+            proj_recv.at[way, half - 1, part],
+            way,
+            1,
+        )
+
     def proj_copy(way, step, part):
         spot = pl.ds(part * rows, rows)
-        return along(
+        return move(
             proj_out.at[way, step, spot],
             proj_in.at[way, step, spot],
             proj_send.at[way, step, part],
             proj_recv.at[way, step, part],
             way,
+            1,
         )
 
     def make_term(target):
@@ -414,42 +413,52 @@
     def far(way, part, parts):
         return (part < parts // 2) == (way == 0)
 
-    def proj_step(step, started):
+    def proj_step(step, first):
         for part in range(CHUNKS):
             for way in range(2):
-                fresh = started == 0 or (started == 1 and not far(way, part, CHUNKS))
-                if started == 0 and not far(way, part, CHUNKS):
-                    continue
                 spot = pl.ds(part * rows, rows)
-                term = proj_term(target_of(way, step), part)
-                if not fresh:
+                term = proj_term(place_at(way, half - 1 - step), part)
+                if first:
+                    proj_near(way, part).wait_recv()
+                    term = term + proj_in[way, half - 1, spot].astype(F32)
+                    if far(way, part, CHUNKS):
+                        proj_far(way, part).wait_recv()
+                        term = term + proj_in[way, 0, spot].astype(F32)
+                else:
                     proj_copy(way, step - 1, part).wait_recv()
                     term = term + proj_in[way, step - 1, spot].astype(F32)
                 proj_out[way, step, spot] = term.astype(BF16)
                 proj_copy(way, step, part).start()
 
-    make_term(target_of(0, 0))
-    proj_step(0, 0)
-    make_term(target_of(0, 1))
-    make_term(target_of(1, 1))
-    proj_step(1, 1)
+    make_term(place_at(0, half))
+    for part in range(CHUNKS):
+        for way in range(2):
+            if far(way, part, CHUNKS):
+                proj_far(way, part).start()
+    for way in range(2):
+        make_term(place_at(way, half - 1))
+        for part in range(CHUNKS):
+            proj_near(way, part).start()
+    for way in range(2):
+        make_term(place_at(way, half - 2))
+    proj_step(1, True)
 
     def proj_loop(step, carry):
-        make_term(target_of(0, step))
-        make_term(target_of(1, step))
-        proj_step(step, 2)
-        for i, stream in enumerate((key_stream, value_stream, *weight_streams)):
+        for way in range(2):
+            make_term(place_at(way, half - 1 - step))
+        proj_step(step, False)
+        for i, stream in enumerate((kv_stream, weight_stream)):
             pl.when(step == 2 + i)(stream.sent)
         return carry
 
-    lax.fori_loop(2, half, proj_loop, 0)
+    lax.fori_loop(2, half - 1, proj_loop, 0)
     make_term(z)
     for part in range(CHUNKS):
         spot = pl.ds(part * rows, rows)
         term = proj_term(z, part)
         for way in range(2):
-            proj_copy(way, half - 1, part).wait_recv()
-            term = term + proj_in[way, half - 1, spot].astype(F32)
+            proj_copy(way, half - 2, part).wait_recv()
+            term = term + proj_in[way, half - 2, spot].astype(F32)
         proj_ref[spot, :] = term.astype(BF16)
 
     packed_ref[...] = dot(pick_ref[...], proj_ref[...]).astype(BF16)
@@ -493,19 +502,6 @@
     piece = share // PARTS
 
     hops = half // 2
-
-    def place_at(way, offset):
-        return lax.rem(z + (offset if way == 0 else n_exp - offset), n_exp)
-
-    def move(source, target, send_sem, recv_sem, way, distance):
-        return pltpu.make_async_remote_copy(
-            src_ref=source,
-            dst_ref=target,
-            send_sem=send_sem,
-            recv_sem=recv_sem,
-            device_id=(me, place_at(way, distance)),
-            device_id_type=pl.DeviceIdType.MESH,
-        )
 
     def part_rows(target, part):
         return pl.ds(pl.multiple_of(target * share + part * piece, piece), piece)
@@ -606,7 +602,7 @@
         if step == 1:
             lax.fori_loop(1, half // 2, sent_proj, 0)
         if step == 2:
-            lax.fori_loop(half // 2, half, sent_proj, 0)
+            lax.fori_loop(half // 2, half - 1, sent_proj, 0)
 
     def wait_sq(r, carry):
         sq_copy(r).wait_recv()
@@ -704,7 +700,8 @@
     for way in range(2):
         for part in range(CHUNKS):
             if far(way, part, CHUNKS):
-                proj_copy(way, 0, part).wait_send()
+                proj_far(way, part).wait_send()
+            proj_near(way, part).wait_send()
     for step in range(hops):
         for way, part in both:
             if hid_far(way, step, part):
@@ -734,7 +731,7 @@
         in_specs=[vmem] * 3 + [anywhere] * 6,
         out_specs=vmem,
         scratch_shapes=[
-            pltpu.VMEM((2, n_ctx, tokens, HD), BF16),
+            pltpu.VMEM((n_ctx, 2, tokens, HD), BF16),
             pltpu.VMEM((n_ctx, *weight.shape), BF16),
             pltpu.VMEM((heads, tokens, 1), F32),
             pltpu.VMEM((heads, tokens, 2 * HD), F32),
@@ -761,8 +758,8 @@
             pltpu.VMEM((lots, local), BF16),
             pltpu.VMEM((lots, local), BF16),
             dma((6,)),
-            dma((4, MESSAGES)),
-            dma((4, MESSAGES)),
+            dma((2, MESSAGES)),
+            dma((2, MESSAGES)),
             dma((2, half, CHUNKS)),
             dma((2, half, CHUNKS)),
             dma((n_ctx,)),

time: 135 us -> 131 us (0.970)
  Pallas kernels: 133 us -> 130 us
    pallas_call x1, Pallas kernels: 133 us -> 130 us  [layer(): pl.pallas_call(functools.partial(layer_kernel, n_ctx, n_exp), out_shape=j...]
where the time goes in v4:
time: 131 us
  Pallas kernels  130 us (99%)
  other arithmetic  1.66 us (1%)
    pallas_call x1, Pallas kernels, layer(): pl.pallas_call(functools.partial(layer_kernel, n_ctx, n_exp), out_shape=j...  130 us

profile of v4, /device:TPU:1, one launch (start us, length us, event | category | flops | bytes accessed | tf_op | source)
XLA Modules:
  0.0 131.2 jit_solution(14072403118796256209)
XLA Ops:
  0.0 0.0 copy-start
  0.0 129.6 %layer.1 = bf16[256,256]{1,0:T(8,128)(2,1)} custom-call(bf16[256,256]{1,0:T(8,128)(2,1)} %bitcast.10, s32[1,256]{1,0:T(1,128)} %bitcast.12, f32[1,256]{1,0:T(1,128)} %bitcast.13, bf16[256,1024]{1,0:T(8,128)(2,1)} %bitcast.8, bf16[256,1024]{1,0:T(8,128)(2,1)} %bitcast.9, bf16[256,128]{1,0:T(8,128)(2,1)} %weight_hbm.1, bf16[4,256,512]{2,1,0:T(8,128)(2,1)} %gate_hbm.1, ...), custom_call_target="tpu_custom_call" | custom-call | tf_op jit(solution)/shard_map/layer/pallas_call | solution.py:728
  129.6 0.0 copy-done
  129.6 1.7 %fusion = bf16[1,256,256]{2,1,0:T(8,128)(2,1)} fusion(bf16[256,256]{1,0:T(8,128)(2,1)} %layer.1, f32[256]{0:T(256)S(1)} %bitcast.11), kind=kLoop, calls=%fused_computation.1 | loop fusion | flops 196608 | bytes 263168 | tf_op jit(solution)/shard_map/broadcast_in_dim | solution.py:810
Async XLA Ops:
  0.0 129.6 %copy-start = (f32[1,256]{1,0:T(1,128)S(1)}, f32[1,256]{1,0:T(1,128)}, u32[]{:S(2)}) copy-start(f32[1,256]{1,0:T(1,128)} %param.14) | copy-start | bytes 3076

commit v5 on v4

--- a/solution.py
+++ b/solution.py
@@ -33,6 +33,7 @@
     n_exp,
     query_ref,
     route_ref,
+    score_ref,
     gain_ref,
     keys_hbm,
     values_hbm,
@@ -93,6 +94,22 @@
     each = lots // n_ctx
     most = each // experts
 
+    barrier = pltpu.get_barrier_semaphore()
+
+    def greet_ctx(r, carry):
+        pl.semaphore_signal(
+            barrier, inc=1, device_id=(lax.rem(me + r, n_ctx), z), device_id_type=pl.DeviceIdType.MESH
+        )
+        return carry
+
+    def greet_exp(r, carry):
+        pl.semaphore_signal(
+            barrier, inc=1, device_id=(me, lax.rem(z + r, n_exp)), device_id_type=pl.DeviceIdType.MESH
+        )
+        return carry
+
+    lax.fori_loop(1, n_ctx, greet_ctx, 0)
+    lax.fori_loop(1, n_exp, greet_exp, 0)
     kv_heads = keys_hbm.shape[1] // HD
     columns = pl.ds(pl.multiple_of(z * kv_heads // n_exp * HD, HD), HD)
     own_loads = [
@@ -110,22 +127,6 @@
     for load in loads:
         load.start()
 
-    barrier = pltpu.get_barrier_semaphore()
-
-    def greet_ctx(r, carry):
-        pl.semaphore_signal(
-            barrier, inc=1, device_id=(lax.rem(me + r, n_ctx), z), device_id_type=pl.DeviceIdType.MESH
-        )
-        return carry
-
-    def greet_exp(r, carry):
-        pl.semaphore_signal(
-            barrier, inc=1, device_id=(me, lax.rem(z + r, n_exp)), device_id_type=pl.DeviceIdType.MESH
-        )
-        return carry
-
-    lax.fori_loop(1, n_ctx, greet_ctx, 0)
-    lax.fori_loop(1, n_exp, greet_exp, 0)
     pl.semaphore_wait(barrier, n_ctx - 1 + n_exp - 1)
 
     lane = me % 2
@@ -260,40 +261,48 @@
     block = 2 * tokens
     factor = math.log2(math.e) / math.sqrt(HD)
 
-    def attend(i, j):
-        own = i == 0 and j == 0
+    def update(sources, own):
+        width = block * len(sources)
+
+        def gathered(which):
+            blocks = [kv_ref[pl.ds(source * 2, 2), which].reshape(block, HD) for source in sources]
+            return jnp.concatenate(blocks, axis=0) if len(blocks) > 1 else blocks[0]
+
+        keys = gathered(0)
+        values = jnp.concatenate([gathered(1), jnp.ones((width, HD), BF16)], axis=1)
+        for head in range(heads):
+            query = query_ref[:, head * HD : (head + 1) * HD]
+            scores = lax.dot_general(
+                query, keys, (((1,), (1,)), ((), ())), preferred_element_type=F32
+            )
+            if own:
+                shape = (tokens, width)
+                spot = lane * tokens + lax.broadcasted_iota(jnp.int32, shape, 0)
+                visible = lax.broadcasted_iota(jnp.int32, shape, 1) <= spot
+                scores = jnp.where(visible, scores, FAR_BELOW)
+            highest = jnp.max(scores, axis=1, keepdims=True)
+            if not own:
+                before = high_ref[head]
+                highest = jnp.maximum(highest, before)
+            weights = jnp.exp2((scores - highest) * factor).astype(BF16)
+            summed = dot(weights, values)
+            if not own:
+                summed = summed + total_ref[head] * jnp.exp2((before - highest) * factor)
+            total_ref[head] = summed
+            high_ref[head] = highest
+
+    def source_of(i, j):
         kv_stream.twin_in(i, j).wait_recv()
-        source = kv_stream.chip(STEPS_OFF[i], STEPS_OFF[j])
-
-        def compute():
-            keys = kv_ref[pl.ds(source * 2, 2), 0].reshape(block, HD)
-            values = kv_ref[pl.ds(source * 2, 2), 1].reshape(block, HD)
-            values = jnp.concatenate([values, jnp.ones((block, HD), BF16)], axis=1)
-            for head in range(heads):
-                query = query_ref[:, head * HD : (head + 1) * HD]
-                scores = lax.dot_general(
-                    query, keys, (((1,), (1,)), ((), ())), preferred_element_type=F32
-                )
-                if own:
-                    shape = (tokens, block)
-                    spot = lane * tokens + lax.broadcasted_iota(jnp.int32, shape, 0)
-                    visible = lax.broadcasted_iota(jnp.int32, shape, 1) <= spot
-                    scores = jnp.where(visible, scores, FAR_BELOW)
-                highest = jnp.max(scores, axis=1, keepdims=True)
-                if not own:
-                    before = high_ref[head]
-                    highest = jnp.maximum(highest, before)
-                weights = jnp.exp2((scores - highest) * factor).astype(BF16)
-                summed = dot(weights, values)
-                if not own:
-                    summed = summed + total_ref[head] * jnp.exp2((before - highest) * factor)
-                total_ref[head] = summed
-                high_ref[head] = highest
-
-        if own:
-            compute()
-        else:
-            pl.when(source < chip)(compute)
+        return kv_stream.chip(STEPS_OFF[i], STEPS_OFF[j])
+
+    def attend(*places):
+        sources = [source_of(i, j) for i, j in places]
+        if len(sources) == 1:
+            pl.when(sources[0] < chip)(lambda: update(sources, False))
+            return
+        low, high = jnp.minimum(*sources), jnp.maximum(*sources)
+        pl.when(high < chip)(lambda: update(sources, False))
+        pl.when(jnp.logical_and(low < chip, high >= chip))(lambda: update([low], False))
 
     in_all = lots // experts
 
@@ -331,20 +340,20 @@
         load.wait()
     stage(0)
     make_tables()
-    attend(0, 0)
+    update([source_of(0, 0)], True)
     stage(1)
     stage(2)
-    for i, j in ((1, 0), (2, 0), (0, 1), (0, 2)):
-        attend(i, j)
+    attend((1, 0), (2, 0))
+    attend((0, 1), (0, 2))
     stage(3)
-    for i, j in ((3, 0), (0, 3)):
-        attend(i, j)
+    attend((3, 0), (0, 3))
+    attend((1, 1), (1, 2))
     stage(4)
-    for i, j in ((1, 1), (1, 2), (2, 1), (2, 2)):
-        attend(i, j)
+    attend((2, 1), (2, 2))
+    attend((3, 1), (3, 2))
     stage(5)
-    for i, j in ((3, 1), (3, 2), (1, 3), (2, 3), (3, 3)):
-        attend(i, j)
+    attend((1, 3), (2, 3))
+    attend((3, 3))
     for head in range(heads):
         summed = total_ref[head]
         attn_ref[:, head * HD : (head + 1) * HD] = (summed[:, :HD] / summed[:, HD:]).astype(BF16)
@@ -615,6 +624,18 @@
     at_row = lax.broadcasted_iota(jnp.int32, (share, HD), 0)
     column = jnp.sum(jnp.where(at_lane == at_row, row, 0.0), axis=1, keepdims=True)
     scale = lax.rsqrt(column / (local * n_exp) + EPS)
+
+    def hid_copy(way, step, part, distance, ahead=0):
+        block = place_at(1 - way, 2 * step + ahead)
+        spot = hidden_ref.at[part_rows(block, part)]
+        lane_of = (2 - distance) * hops + step
+        return move(
+            spot, spot, hid_send.at[way, lane_of, part], hid_recv.at[way, lane_of, part], way, distance
+        )
+
+    def hid_far(way, step, part):
+        return step < hops - 1 or far(way, part, PARTS)
+
     for part in range(PARTS):
         term = gu_term(z, part)
         for way in range(2):
@@ -622,26 +643,18 @@
         term = term * scale[part * piece : (part + 1) * piece]
         gate, upper = term[:, :units], term[:, units:]
         hidden = gate / (1.0 + jnp.exp(-gate)) * upper
-        hidden_ref[pl.ds(pl.multiple_of(z * share + part * piece, piece), piece), :] = hidden.astype(BF16)
-
-    def hid_copy(way, step, part, distance, ahead=0):
-        block = place_at(1 - way, 2 * step + ahead)
-        spot = hidden_ref.at[part_rows(block, part)]
-        lane_of = (2 - distance) * hops + step
-        return move(
-            spot, spot, hid_send.at[way, lane_of, part], hid_recv.at[way, lane_of, part], way, distance
-        )
-
-    def hid_far(way, step, part):
-        return step < hops - 1 or far(way, part, PARTS)
+        hidden_ref[part_rows(z, part), :] = hidden.astype(BF16)
+        for way in range(2):
+            hid_copy(way, 0, part, 2).start()
+            hid_copy(way, 0, part, 1).start()
 
     for step in range(hops):
         for way, part in both:
             if step > 0:
                 hid_copy(way, step - 1, part, 2, 2).wait_recv()
-            if hid_far(way, step, part):
-                hid_copy(way, step, part, 2).start()
-            hid_copy(way, step, part, 1).start()
+                if hid_far(way, step, part):
+                    hid_copy(way, step, part, 2).start()
+                hid_copy(way, step, part, 1).start()
         if step == 0:
             for way, part in both:
                 if far(way, part, PARTS):
@@ -709,12 +722,16 @@
             hid_copy(way, step, part, 1).wait_send()
     lax.fori_loop(1, n_exp, sent_exp, 0)
     lax.fori_loop(1, n_ctx, sent_ctx, 0)
+    square = (tokens, tokens)
+    at_row = lax.broadcasted_iota(jnp.int32, square, 0)
+    at_lane = lax.broadcasted_iota(jnp.int32, square, 1)
+    score = jnp.sum(jnp.where(at_row == at_lane, score_ref[...], 0.0), axis=1, keepdims=True)
     lax.fori_loop(1, n_ctx, wait_home, 0)
-    out_ref[...] = dot(spread_ref[...], back_ref[...]).astype(BF16)
+    out_ref[...] = (dot(spread_ref[...], back_ref[...]) * score).astype(BF16)
     lax.fori_loop(1, n_ctx, sent_home, 0)
 
 
-def layer(n_ctx, n_exp, query, route, gain, keys, values, weight, gate, up, down):
+def layer(n_ctx, n_exp, query, route, score, gain, keys, values, weight, gate, up, down):
     tokens, local = query.shape
     experts, _, units = gate.shape
     most = 2 * tokens // (experts * n_ctx)
@@ -728,7 +745,7 @@
     return pl.pallas_call(
         functools.partial(layer_kernel, n_ctx, n_exp),
         out_shape=jax.ShapeDtypeStruct((tokens, local), BF16),
-        in_specs=[vmem] * 3 + [anywhere] * 6,
+        in_specs=[vmem] * 4 + [anywhere] * 6,
         out_specs=vmem,
         scratch_shapes=[
             pltpu.VMEM((n_ctx, 2, tokens, HD), BF16),
@@ -777,7 +794,7 @@
             collective_id=0, has_side_effects=True, vmem_limit_bytes=VMEM_LIMIT
         ),
         name="layer",
-    )(query, route, gain, keys, values, weight, gate, up, down)
+    )(query, route, score, gain, keys, values, weight, gate, up, down)
 
 
 def body(
@@ -793,11 +810,12 @@
     down_weight,
 ):
     tokens, local = queries.shape[1:]
-    returned = layer(
+    return layer(
         lax.axis_size("ctx"),
         lax.axis_size("exp"),
         queries[0],
         routes[0].reshape(1, tokens),
+        route_score,
         norm_gain.reshape(1, local),
         keys[0],
         values[0],
@@ -805,9 +823,7 @@
         gate_weight,
         up_weight,
         down_weight,
-    )
-    scored = route_score[0][:, None] * returned.astype(F32)
-    return scored.astype(BF16)[None]
+    )[None]
 
 
 def solution(mesh):

time: 131 us -> 127 us (0.969)
  Pallas kernels: 130 us -> 126 us
  other arithmetic: 1.66 us -> 0 us
  local copies, waits for them, and re-layouts: 0.01 us -> 1.57 us
    pallas_call x1, Pallas kernels: 130 us -> 126 us  [layer(): pl.pallas_call(functools.partial(layer_kernel, n_ctx, n_exp), out_shape=j...]
    broadcast_in_dim x1 -> x0, other arithmetic: 1.66 us -> none  [body(): return scored.astype(BF16)[None]]
    unnamed x2 -> x1, local copies, waits for them, and re-layouts: 0.01 us -> 1.57 us
where the time goes in v5:
time: 127 us
  Pallas kernels  126 us (99%)
  local copies, waits for them, and re-layouts  1.57 us (1%)
    pallas_call x1, Pallas kernels, layer(): pl.pallas_call(functools.partial(layer_kernel, n_ctx, n_exp), out_shape=j...  126 us

profile of v5, /device:TPU:1, one launch (start us, length us, event | category | flops | bytes accessed | tf_op | source)
XLA Modules:
  0.0 127.2 jit_solution(15899322351149154492)
XLA Ops:
  0.0 125.7 %layer.1 = bf16[256,256]{1,0:T(8,128)(2,1)} custom-call(bf16[256,256]{1,0:T(8,128)(2,1)} %bitcast.9, s32[1,256]{1,0:T(1,128)} %bitcast.10, f32[1,256]{1,0:T(1,128)} %score_ref.1, f32[1,256]{1,0:T(1,128)} %bitcast.11, bf16[256,1024]{1,0:T(8,128)(2,1)} %bitcast.6, bf16[256,1024]{1,0:T(8,128)(2,1)} %bitcast.7, bf16[256,128]{1,0:T(8,128)(2,1)} %weight_hbm.1, ...), custom_call_target="tpu_custom_call" | custom-call | tf_op jit(solution)/shard_map/layer/pallas_call | solution.py:745
  125.7 1.6 %copy.12 = bf16[1,256,256]{2,1,0:T(8,128)(2,1)} copy(bf16[1,256,256]{2,1,0:T(8,128)(2,1)} %bitcast.8) | data formatting | bytes 262144

commit v6 on v5

--- a/solution.py
+++ b/solution.py
@@ -472,6 +472,9 @@
 
     packed_ref[...] = dot(pick_ref[...], proj_ref[...]).astype(BF16)
 
+    def far_first(r):
+        return 1 + lax.rem(r + n_ctx // 3, n_ctx - 1)
+
     def there_copy(r):
         peer = lax.rem(me + r, n_ctx)
         return pltpu.make_async_remote_copy(
@@ -484,7 +487,7 @@
         )
 
     def start_there(r, carry):
-        there_copy(r).start()
+        there_copy(far_first(r)).start()
         return carry
 
     def wait_there(r, carry):
@@ -514,6 +517,9 @@
 
     def part_rows(target, part):
         return pl.ds(pl.multiple_of(target * share + part * piece, piece), piece)
+
+    stops = (*range(half, 2, -2), 2, 1, 0)
+    long_hops = len(stops) - 3
 
     def gu_chain(way, step, part):
         spot = pl.ds(part * piece, piece)
@@ -527,16 +533,17 @@
             gu_send.at[way, step, part],
             gu_recv.at[way, step, part],
             way,
-            2,
+            stops[step] - stops[step + 1],
         )
 
     def gu_leaf(way, step, part):
         spot = pl.ds(part * piece, piece)
+        slot = len(stops) - 1 + step
         return move(
-            part_ref.at[part_rows(place_at(way, half - 1 - 2 * step), part)],
-            gu_in.at[way, hops + step, spot],
-            gu_send.at[way, hops + step, part],
-            gu_recv.at[way, hops + step, part],
+            part_ref.at[part_rows(place_at(way, stops[step] - 1), part)],
+            gu_in.at[way, slot, spot],
+            gu_send.at[way, slot, part],
+            gu_recv.at[way, slot, part],
             way,
             1,
         )
@@ -546,8 +553,9 @@
 
     def gu_arrived(term, way, step, part):
         spot = pl.ds(part * piece, piece)
-        gu_leaf(way, step, part).wait_recv()
-        term = term + gu_in[way, hops + step, spot].astype(F32)
+        if step < long_hops:
+            gu_leaf(way, step, part).wait_recv()
+            term = term + gu_in[way, len(stops) - 1 + step, spot].astype(F32)
         if step > 0 or far(way, part, PARTS):
             gu_chain(way, step, part).wait_recv()
             term = term + gu_in[way, step, spot].astype(F32)
@@ -560,9 +568,10 @@
             gu_leaf(way, step, part).start()
 
     def gu_step(step):
-        gu_leaves(step)
+        if step < long_hops:
+            gu_leaves(step)
         for way, part in both:
-            term = gu_arrived(gu_term(place_at(way, half - 2 * step), part), way, step - 1, part)
+            term = gu_arrived(gu_term(place_at(way, stops[step]), part), way, step - 1, part)
             gu_out[way, step, pl.ds(part * piece, piece)] = term.astype(BF16)
             gu_chain(way, step, part).start()
 
@@ -606,7 +615,7 @@
                 proj_copy(way, step, part).wait_send()
         return carry
 
-    for step in range(1, hops):
+    for step in range(1, len(stops) - 1):
         gu_step(step)
         if step == 1:
             lax.fori_loop(1, half // 2, sent_proj, 0)
@@ -639,7 +648,7 @@
     for part in range(PARTS):
         term = gu_term(z, part)
         for way in range(2):
-            term = gu_arrived(term, way, hops - 1, part)
+            term = gu_arrived(term, way, len(stops) - 2, part)
         term = term * scale[part * piece : (part + 1) * piece]
         gate, upper = term[:, :units], term[:, units:]
         hidden = gate / (1.0 + jnp.exp(-gate)) * upper
@@ -655,14 +664,10 @@
                 if hid_far(way, step, part):
                     hid_copy(way, step, part, 2).start()
                 hid_copy(way, step, part, 1).start()
-        if step == 0:
-            for way, part in both:
-                if far(way, part, PARTS):
-                    gu_chain(way, 0, part).wait_send()
-                gu_leaf(way, 0, part).wait_send()
-        else:
-            for way, part in both:
+        for way, part in both:
+            if step > 0 or far(way, part, PARTS):
                 gu_chain(way, step, part).wait_send()
+            if step < long_hops:
                 gu_leaf(way, step, part).wait_send()
     for step in range(hops):
         for way, part in both:
@@ -688,7 +693,7 @@
         )
 
     def start_home(r, carry):
-        home_copy(r).start()
+        home_copy(far_first(r)).start()
         return carry
 
     def wait_home(r, carry):
@@ -715,6 +720,9 @@
             if far(way, part, CHUNKS):
                 proj_far(way, part).wait_send()
             proj_near(way, part).wait_send()
+    for step in range(hops, len(stops) - 1):
+        for way, part in both:
+            gu_chain(way, step, part).wait_send()
     for step in range(hops):
         for way, part in both:
             if hid_far(way, step, part):

time: 127 us -> 129 us (1.016)
    pallas_call x1, Pallas kernels: 126 us -> 127 us  [layer(): pl.pallas_call(functools.partial(layer_kernel, n_ctx, n_exp), out_shape=j...]
where the time goes in v6:
time: 129 us
  Pallas kernels  127 us (98%)
  local copies, waits for them, and re-layouts  1.57 us (1%)
    pallas_call x1, Pallas kernels, layer(): pl.pallas_call(functools.partial(layer_kernel, n_ctx, n_exp), out_shape=j...  127 us

profile of v6, /device:TPU:1, one launch (start us, length us, event | category | flops | bytes accessed | tf_op | source)
XLA Modules:
  0.0 129.0 jit_solution(14813036584379877662)
XLA Ops:
  0.0 127.4 %layer.1 = bf16[256,256]{1,0:T(8,128)(2,1)} custom-call(bf16[256,256]{1,0:T(8,128)(2,1)} %bitcast.9, s32[1,256]{1,0:T(1,128)} %bitcast.10, f32[1,256]{1,0:T(1,128)} %score_ref.1, f32[1,256]{1,0:T(1,128)} %bitcast.11, bf16[256,1024]{1,0:T(8,128)(2,1)} %bitcast.6, bf16[256,1024]{1,0:T(8,128)(2,1)} %bitcast.7, bf16[256,128]{1,0:T(8,128)(2,1)} %weight_hbm.1, ...), custom_call_target="tpu_custom_call" | custom-call | tf_op jit(solution)/shard_map/layer/pallas_call | solution.py:753
  127.4 1.6 %copy.12 = bf16[1,256,256]{2,1,0:T(8,128)(2,1)} copy(bf16[1,256,256]{2,1,0:T(8,128)(2,1)} %bitcast.8) | data formatting | bytes 262144

commit v7 on v5

--- a/solution.py
+++ b/solution.py
@@ -377,29 +377,10 @@
             device_id_type=pl.DeviceIdType.MESH,
         )
 
-    def proj_far(way, part):
-        spot = pl.ds(part * rows, rows)
-        return move(
-            term_ref.at[place_at(way, half), spot],
-            proj_in.at[way, 0, spot],
-            proj_send.at[way, 0, part],
-            proj_recv.at[way, 0, part],
-            way,
-            2,
-        )
-
-    def proj_near(way, part):
-        spot = pl.ds(part * rows, rows)
-        return move(
-            term_ref.at[place_at(way, half - 1), spot],
-            proj_in.at[way, half - 1, spot],
-            proj_send.at[way, half - 1, part],
-            proj_recv.at[way, half - 1, part],
-            way,
-            1,
-        )
-
-    def proj_copy(way, step, part):
+    long_hops = 2
+    last = half - 1 - long_hops
+
+    def proj_copy(way, step, part, distance=1):
         spot = pl.ds(part * rows, rows)
         return move(
             proj_out.at[way, step, spot],
@@ -407,8 +388,25 @@
             proj_send.at[way, step, part],
             proj_recv.at[way, step, part],
             way,
-            1,
-        )
+            distance,
+        )
+
+    def proj_term_copy(way, offset, slot, part, distance):
+        spot = pl.ds(part * rows, rows)
+        return move(
+            term_ref.at[place_at(way, offset), spot],
+            proj_in.at[way, slot, spot],
+            proj_send.at[way, slot, part],
+            proj_recv.at[way, slot, part],
+            way,
+            distance,
+        )
+
+    def proj_far(way, part):
+        return proj_term_copy(way, half, 0, part, 2)
+
+    def proj_near(way, step, part):
+        return proj_term_copy(way, half - 1 - 2 * step, last + 1 + step, part, 1)
 
     def make_term(target):
         columns = jnp.concatenate(
@@ -422,52 +420,62 @@
     def far(way, part, parts):
         return (part < parts // 2) == (way == 0)
 
-    def proj_step(step, first):
+    def proj_step(step, offset):
         for part in range(CHUNKS):
             for way in range(2):
                 spot = pl.ds(part * rows, rows)
-                term = proj_term(place_at(way, half - 1 - step), part)
-                if first:
-                    proj_near(way, part).wait_recv()
-                    term = term + proj_in[way, half - 1, spot].astype(F32)
-                    if far(way, part, CHUNKS):
-                        proj_far(way, part).wait_recv()
-                        term = term + proj_in[way, 0, spot].astype(F32)
-                else:
+                term = proj_term(place_at(way, offset), part)
+                side = isinstance(step, int) and step <= long_hops
+                if side:
+                    proj_near(way, step - 1, part).wait_recv()
+                    term = term + proj_in[way, last + step, spot].astype(F32)
+                if not side or step > 1:
                     proj_copy(way, step - 1, part).wait_recv()
                     term = term + proj_in[way, step - 1, spot].astype(F32)
+                elif far(way, part, CHUNKS):
+                    proj_far(way, part).wait_recv()
+                    term = term + proj_in[way, 0, spot].astype(F32)
                 proj_out[way, step, spot] = term.astype(BF16)
-                proj_copy(way, step, part).start()
+                proj_copy(way, step, part, 2 if side and step < long_hops else 1).start()
+
+    def make_terms(offset):
+        for way in range(2):
+            make_term(place_at(way, offset))
+
+    def start_near(step):
+        for part in range(CHUNKS):
+            for way in range(2):
+                proj_near(way, step, part).start()
 
     make_term(place_at(0, half))
     for part in range(CHUNKS):
         for way in range(2):
             if far(way, part, CHUNKS):
                 proj_far(way, part).start()
-    for way in range(2):
-        make_term(place_at(way, half - 1))
-        for part in range(CHUNKS):
-            proj_near(way, part).start()
-    for way in range(2):
-        make_term(place_at(way, half - 2))
-    proj_step(1, True)
+    make_terms(half - 1)
+    start_near(0)
+    make_terms(half - 2)
+    make_terms(half - 3)
+    start_near(1)
+    proj_step(1, half - 2)
+    make_terms(half - 4)
+    kv_stream.sent()
+    proj_step(2, half - 4)
 
     def proj_loop(step, carry):
-        for way in range(2):
-            make_term(place_at(way, half - 1 - step))
-        proj_step(step, False)
-        for i, stream in enumerate((kv_stream, weight_stream)):
-            pl.when(step == 2 + i)(stream.sent)
-        return carry
-
-    lax.fori_loop(2, half - 1, proj_loop, 0)
+        make_terms(last + 1 - step)
+        proj_step(step, last + 1 - step)
+        return carry
+
+    lax.fori_loop(long_hops + 1, last + 1, proj_loop, 0)
+    weight_stream.sent()
     make_term(z)
     for part in range(CHUNKS):
         spot = pl.ds(part * rows, rows)
         term = proj_term(z, part)
         for way in range(2):
-            proj_copy(way, half - 2, part).wait_recv()
-            term = term + proj_in[way, half - 2, spot].astype(F32)
+            proj_copy(way, last, part).wait_recv()
+            term = term + proj_in[way, last, spot].astype(F32)
         proj_ref[spot, :] = term.astype(BF16)
 
     packed_ref[...] = dot(pick_ref[...], proj_ref[...]).astype(BF16)
@@ -609,9 +617,9 @@
     for step in range(1, hops):
         gu_step(step)
         if step == 1:
-            lax.fori_loop(1, half // 2, sent_proj, 0)
+            lax.fori_loop(1, long_hops + 1, sent_proj, 0)
         if step == 2:
-            lax.fori_loop(half // 2, half - 1, sent_proj, 0)
+            lax.fori_loop(long_hops + 1, last + 1, sent_proj, 0)
 
     def wait_sq(r, carry):
         sq_copy(r).wait_recv()
@@ -625,16 +633,18 @@
     column = jnp.sum(jnp.where(at_lane == at_row, row, 0.0), axis=1, keepdims=True)
     scale = lax.rsqrt(column / (local * n_exp) + EPS)
 
+    strides = 3
+
     def hid_copy(way, step, part, distance, ahead=0):
-        block = place_at(1 - way, 2 * step + ahead)
+        block = place_at(1 - way, 3 * step + ahead)
         spot = hidden_ref.at[part_rows(block, part)]
-        lane_of = (2 - distance) * hops + step
-        return move(
-            spot, spot, hid_send.at[way, lane_of, part], hid_recv.at[way, lane_of, part], way, distance
-        )
-
-    def hid_far(way, step, part):
-        return step < hops - 1 or far(way, part, PARTS)
+        slot = step + (0, 2, 5, 0)[distance]
+        return move(spot, spot, hid_send.at[way, slot, part], hid_recv.at[way, slot, part], way, distance)
+
+    def hid_distances(way, step, part):
+        if step < strides - 1:
+            return (3, 2, 1)
+        return (2, 1) if far(way, part, PARTS) else (1,)
 
     for part in range(PARTS):
         term = gu_term(z, part)
@@ -645,31 +655,24 @@
         hidden = gate / (1.0 + jnp.exp(-gate)) * upper
         hidden_ref[part_rows(z, part), :] = hidden.astype(BF16)
         for way in range(2):
-            hid_copy(way, 0, part, 2).start()
-            hid_copy(way, 0, part, 1).start()
-
-    for step in range(hops):
+            for distance in hid_distances(way, 0, part):
+                hid_copy(way, 0, part, distance).start()
+
+    for step in range(strides):
         for way, part in both:
             if step > 0:
-                hid_copy(way, step - 1, part, 2, 2).wait_recv()
-                if hid_far(way, step, part):
-                    hid_copy(way, step, part, 2).start()
-                hid_copy(way, step, part, 1).start()
-        if step == 0:
-            for way, part in both:
-                if far(way, part, PARTS):
-                    gu_chain(way, 0, part).wait_send()
-                gu_leaf(way, 0, part).wait_send()
-        else:
-            for way, part in both:
+                hid_copy(way, step - 1, part, 3, 3).wait_recv()
+                for distance in hid_distances(way, step, part):
+                    hid_copy(way, step, part, distance).start()
+        for way, part in both:
+            if step > 0 or far(way, part, PARTS):
                 gu_chain(way, step, part).wait_send()
-                gu_leaf(way, step, part).wait_send()
-    for step in range(hops):
+            gu_leaf(way, step, part).wait_send()
+    for step in range(strides):
         for way, part in both:
-            hid_copy(way, step, part, 1, 1).wait_recv()
-    for way, part in both:
-        if hid_far(way, hops - 1, part):
-            hid_copy(way, hops - 1, part, 2, 2).wait_recv()
+            for distance in hid_distances(way, step, part):
+                if distance < 3:
+                    hid_copy(way, step, part, distance, distance).wait_recv()
 
     made = jnp.concatenate(
         [dot(hidden_ref[pl.ds(e * in_all, in_all), :], down_ref[e]) for e in range(experts)], axis=0
@@ -714,12 +717,15 @@
         for part in range(CHUNKS):
             if far(way, part, CHUNKS):
                 proj_far(way, part).wait_send()
-            proj_near(way, part).wait_send()
-    for step in range(hops):
+            for step in range(long_hops):
+                proj_near(way, step, part).wait_send()
+    for way, part in both:
+        gu_chain(way, hops - 1, part).wait_send()
+        gu_leaf(way, hops - 1, part).wait_send()
+    for step in range(strides):
         for way, part in both:
-            if hid_far(way, step, part):
-                hid_copy(way, step, part, 2).wait_send()
-            hid_copy(way, step, part, 1).wait_send()
+            for distance in hid_distances(way, step, part):
+                hid_copy(way, step, part, distance).wait_send()
     lax.fori_loop(1, n_exp, sent_exp, 0)
     lax.fori_loop(1, n_ctx, sent_ctx, 0)
     square = (tokens, tokens)

time: 127 us -> 128 us (level)
  no operation moved by 1% of the time
where the time goes in v7:
time: 128 us
  Pallas kernels  127 us (99%)
  local copies, waits for them, and re-layouts  1.57 us (1%)
    pallas_call x1, Pallas kernels, layer(): pl.pallas_call(functools.partial(layer_kernel, n_ctx, n_exp), out_shape=j...  127 us

profile of v7, /device:TPU:1, one launch (start us, length us, event | category | flops | bytes accessed | tf_op | source)
XLA Modules:
  0.0 128.3 jit_solution(18424478065337570384)
XLA Ops:
  0.0 126.7 %layer.1 = bf16[256,256]{1,0:T(8,128)(2,1)} custom-call(bf16[256,256]{1,0:T(8,128)(2,1)} %bitcast.9, s32[1,256]{1,0:T(1,128)} %bitcast.10, f32[1,256]{1,0:T(1,128)} %score_ref.1, f32[1,256]{1,0:T(1,128)} %bitcast.11, bf16[256,1024]{1,0:T(8,128)(2,1)} %bitcast.6, bf16[256,1024]{1,0:T(8,128)(2,1)} %bitcast.7, bf16[256,128]{1,0:T(8,128)(2,1)} %weight_hbm.1, ...), custom_call_target="tpu_custom_call" | custom-call | tf_op jit(solution)/shard_map/layer/pallas_call | solution.py:751
  126.7 1.6 %copy.12 = bf16[1,256,256]{2,1,0:T(8,128)(2,1)} copy(bf16[1,256,256]{2,1,0:T(8,128)(2,1)} %bitcast.8) | data formatting | bytes 262144

commit v8 on v5

--- a/solution.py
+++ b/solution.py
@@ -23,6 +23,7 @@
 NX = 4
 NY = 4
 STEPS_OFF = (0, 1, -1, 2)
+ONES = 16
 MESSAGES = 36
 CHUNKS = 4
 PARTS = 2
@@ -44,6 +45,8 @@
     out_ref,
     kv_ref,
     weight_ref,
+    value_ref,
+    across_ref,
     high_ref,
     total_ref,
     attn_ref,
@@ -114,7 +117,7 @@
     columns = pl.ds(pl.multiple_of(z * kv_heads // n_exp * HD, HD), HD)
     own_loads = [
         pltpu.make_async_copy(keys_hbm.at[:, columns], kv_ref.at[me, 0], load_sem.at[3]),
-        pltpu.make_async_copy(values_hbm.at[:, columns], kv_ref.at[me, 1], load_sem.at[4]),
+        pltpu.make_async_copy(values_hbm.at[:, columns], value_ref, load_sem.at[4]),
         pltpu.make_async_copy(weight_hbm, weight_ref.at[me], load_sem.at[5]),
     ]
     for load in own_loads:
@@ -126,6 +129,16 @@
     ]
     for load in loads:
         load.start()
+
+    heads = local // HD
+    for head in range(heads):
+        query = query_ref[:, head * HD : (head + 1) * HD].astype(F32)
+        across_ref[head] = query.T.astype(BF16)
+    for load in own_loads:
+        load.wait()
+    for square in range(tokens // HD):
+        spot = pl.ds(square * HD, HD)
+        kv_ref[me, 1, spot, :] = value_ref[spot, :].astype(F32).T.astype(BF16)
 
     pl.semaphore_wait(barrier, n_ctx - 1 + n_exp - 1)
 
@@ -257,35 +270,37 @@
         kv_stream.stage(number)
         weight_stream.stage(number)
 
-    heads = local // HD
     block = 2 * tokens
     factor = math.log2(math.e) / math.sqrt(HD)
 
     def update(sources, own):
         width = block * len(sources)
 
-        def gathered(which):
-            blocks = [kv_ref[pl.ds(source * 2, 2), which].reshape(block, HD) for source in sources]
-            return jnp.concatenate(blocks, axis=0) if len(blocks) > 1 else blocks[0]
-
-        keys = gathered(0)
-        values = jnp.concatenate([gathered(1), jnp.ones((width, HD), BF16)], axis=1)
+        keys = jnp.concatenate(
+            [kv_ref[source * 2 + core, 0] for source in sources for core in range(2)], axis=0
+        )
+        squares = [
+            kv_ref[source * 2 + core, 1, pl.ds(square * HD, HD), :]
+            for source in sources
+            for core in range(2)
+            for square in range(tokens // HD)
+        ]
+        values = jnp.concatenate(
+            [jnp.concatenate(squares, axis=1), jnp.ones((ONES, width), BF16)], axis=0
+        )
         for head in range(heads):
-            query = query_ref[:, head * HD : (head + 1) * HD]
-            scores = lax.dot_general(
-                query, keys, (((1,), (1,)), ((), ())), preferred_element_type=F32
-            )
+            scores = dot(keys, across_ref[head])
             if own:
-                shape = (tokens, width)
-                spot = lane * tokens + lax.broadcasted_iota(jnp.int32, shape, 0)
-                visible = lax.broadcasted_iota(jnp.int32, shape, 1) <= spot
+                shape = (width, tokens)
+                spot = lane * tokens + lax.broadcasted_iota(jnp.int32, shape, 1)
+                visible = lax.broadcasted_iota(jnp.int32, shape, 0) <= spot
                 scores = jnp.where(visible, scores, FAR_BELOW)
-            highest = jnp.max(scores, axis=1, keepdims=True)
+            highest = jnp.max(scores, axis=0, keepdims=True)
             if not own:
                 before = high_ref[head]
                 highest = jnp.maximum(highest, before)
             weights = jnp.exp2((scores - highest) * factor).astype(BF16)
-            summed = dot(weights, values)
+            summed = dot(values, weights)
             if not own:
                 summed = summed + total_ref[head] * jnp.exp2((before - highest) * factor)
             total_ref[head] = summed
@@ -336,8 +351,6 @@
         place = (lot % in_all) // most * each + lot // in_all * most + lot % most
         by_device_ref[...] = jnp.where(to_row == place, 1.0, 0.0).astype(BF16)
 
-    for load in own_loads:
-        load.wait()
     stage(0)
     make_tables()
     update([source_of(0, 0)], True)
@@ -356,7 +369,8 @@
     attend((3, 3))
     for head in range(heads):
         summed = total_ref[head]
-        attn_ref[:, head * HD : (head + 1) * HD] = (summed[:, :HD] / summed[:, HD:]).astype(BF16)
+        weighted = summed[:HD] / summed[HD : HD + 1]
+        attn_ref[:, head * HD : (head + 1) * HD] = weighted.T.astype(BF16)
     for i in range(4):
         for j in range(4):
             weight_stream.twin_in(i, j).wait_recv()
@@ -750,8 +764,10 @@
         scratch_shapes=[
             pltpu.VMEM((n_ctx, 2, tokens, HD), BF16),
             pltpu.VMEM((n_ctx, *weight.shape), BF16),
-            pltpu.VMEM((heads, tokens, 1), F32),
-            pltpu.VMEM((heads, tokens, 2 * HD), F32),
+            pltpu.VMEM((tokens, HD), BF16),
+            pltpu.VMEM((heads, HD, tokens), BF16),
+            pltpu.VMEM((heads, 1, tokens), F32),
+            pltpu.VMEM((heads, HD + ONES, tokens), F32),
             pltpu.VMEM((tokens, local), BF16),
             pltpu.VMEM((experts, local, 2 * units), BF16),
             pltpu.VMEM((experts, units, local), BF16),

time: 127 us -> 128 us (level)
  no operation moved by 1% of the time
where the time goes in v8:
time: 128 us
  Pallas kernels  127 us (99%)
  local copies, waits for them, and re-layouts  1.57 us (1%)
    pallas_call x1, Pallas kernels, layer(): pl.pallas_call(functools.partial(layer_kernel, n_ctx, n_exp), out_shape=j...  127 us

profile of v8, /device:TPU:1, one launch (start us, length us, event | category | flops | bytes accessed | tf_op | source)
XLA Modules:
  0.0 128.3 jit_solution(17828121959618479633)
XLA Ops:
  0.0 126.7 %layer.1 = bf16[256,256]{1,0:T(8,128)(2,1)} custom-call(bf16[256,256]{1,0:T(8,128)(2,1)} %bitcast.9, s32[1,256]{1,0:T(1,128)} %bitcast.10, f32[1,256]{1,0:T(1,128)} %score_ref.1, f32[1,256]{1,0:T(1,128)} %bitcast.11, bf16[256,1024]{1,0:T(8,128)(2,1)} %bitcast.6, bf16[256,1024]{1,0:T(8,128)(2,1)} %bitcast.7, bf16[256,128]{1,0:T(8,128)(2,1)} %weight_hbm.1, ...), custom_call_target="tpu_custom_call" | custom-call | tf_op jit(solution)/shard_map/layer/pallas_call | solution.py:759
  126.7 1.6 %copy.12 = bf16[1,256,256]{2,1,0:T(8,128)(2,1)} copy(bf16[1,256,256]{2,1,0:T(8,128)(2,1)} %bitcast.8) | data formatting | bytes 262144

commit v9 on v5

--- a/solution.py
+++ b/solution.py
@@ -59,7 +59,7 @@
     by_device_ref,
     packed_ref,
     arrived_ref,
-    scaled_ref,
+    squared_ref,
     part_ref,
     gu_out,
     gu_in,
@@ -472,6 +472,9 @@
 
     packed_ref[...] = dot(pick_ref[...], proj_ref[...]).astype(BF16)
 
+    def far_first(r):
+        return 1 + lax.rem(r + n_ctx // 3, n_ctx - 1)
+
     def there_copy(r):
         peer = lax.rem(me + r, n_ctx)
         return pltpu.make_async_remote_copy(
@@ -484,7 +487,7 @@
         )
 
     def start_there(r, carry):
-        there_copy(r).start()
+        there_copy(far_first(r)).start()
         return carry
 
     def wait_there(r, carry):
@@ -499,14 +502,15 @@
     lax.fori_loop(1, n_ctx, wait_there, 0)
 
     share = lots // n_exp
-    tokens_in = dot(by_expert_ref[...], arrived_ref[...])
-    scaled_ref[...] = (tokens_in * gain_ref[...]).astype(BF16)
     first_expert = lax.rem(z + half, n_exp) * share // in_all
 
     def make_part(i):
         e = lax.rem(first_expert + i, experts)
         spot = pl.ds(pl.multiple_of(e * in_all, in_all), in_all)
-        part_ref[spot, :] = dot(scaled_ref[spot, :], gu_ref[e]).astype(BF16)
+        tokens_in = dot(by_expert_ref[spot, :], arrived_ref[...])
+        scaled = (tokens_in * gain_ref[...]).astype(BF16)
+        part_ref[spot, :] = dot(scaled, gu_ref[e]).astype(BF16)
+        squared_ref[spot, :] = (tokens_in * tokens_in).astype(BF16)
 
     piece = share // PARTS
 
@@ -576,7 +580,7 @@
 
     squares = lax.dot_general(
         jnp.ones((8, local), BF16),
-        (tokens_in * tokens_in).astype(BF16),
+        squared_ref[...],
         (((1,), (1,)), ((), ())),
         preferred_element_type=F32,
     )
@@ -688,7 +692,7 @@
         )
 
     def start_home(r, carry):
-        home_copy(r).start()
+        home_copy(far_first(r)).start()
         return carry
 
     def wait_home(r, carry):

time: 127 us -> 127 us (level)
  no operation moved by 1% of the time
where the time goes in v9:
time: 127 us
  Pallas kernels  125 us (98%)
  local copies, waits for them, and re-layouts  1.57 us (1%)
    pallas_call x1, Pallas kernels, layer(): pl.pallas_call(functools.partial(layer_kernel, n_ctx, n_exp), out_shape=j...  125 us

profile of v9, /device:TPU:1, one launch (start us, length us, event | category | flops | bytes accessed | tf_op | source)
XLA Modules:
  0.0 126.7 jit_solution(14912005344580479913)
XLA Ops:
  0.0 125.1 %layer.1 = bf16[256,256]{1,0:T(8,128)(2,1)} custom-call(bf16[256,256]{1,0:T(8,128)(2,1)} %bitcast.9, s32[1,256]{1,0:T(1,128)} %bitcast.10, f32[1,256]{1,0:T(1,128)} %score_ref.1, f32[1,256]{1,0:T(1,128)} %bitcast.11, bf16[256,1024]{1,0:T(8,128)(2,1)} %bitcast.6, bf16[256,1024]{1,0:T(8,128)(2,1)} %bitcast.7, bf16[256,128]{1,0:T(8,128)(2,1)} %weight_hbm.1, ...), custom_call_target="tpu_custom_call" | custom-call | tf_op jit(solution)/shard_map/layer/pallas_call | solution.py:749
  125.1 1.6 %copy.12 = bf16[1,256,256]{2,1,0:T(8,128)(2,1)} copy(bf16[1,256,256]{2,1,0:T(8,128)(2,1)} %bitcast.8) | data formatting | bytes 262144
